TPU v7x, 512 devices: a whole 4x4x16 slice. The times are simulated.
512 devices in a mesh: img: 16 (over x, z_hi, core), txt: 32 (over y, z_lo).
Axes of the slice: x: 4, y: 4, z: 16 (z_hi: 2, z_lo: 8; z = z_hi * 8 + z_lo), core: 2. Of those that a mesh axis runs over, the one named last changes fastest.
Arguments:
- images: bfloat16 [9216, 1152], P(('img', 'txt')), may hold values from -8 to 8
- texts: bfloat16 [9216, 1152], P('txt', 'img'), may hold values from -8 to 8
- logit_scale: float32 [1], replicated, may hold values from 48 to 115
- bias: float32 [1], replicated, may hold values from -40 to 0
Outputs:
- loss: float32 [1], replicated
- grad_images: float32 [9216, 1152], P(('img', 'txt'))
- grad_texts: float32 [9216, 1152], P('txt', 'img')
All inputs are finite; a program needn't handle non-finite values.
Results may differ from a plain program's by a relative error of at most 0.033.
Values may be sent and summed in bfloat16 or wider, within the bound.
A program may use at most 64 MiB of HBM per device.

v0:
```python
import jax
import jax.numpy as jnp
from jax import lax
from jax.sharding import PartitionSpec as P

EPS = 1e-06


def per_device(images, texts, logit_scale, bias):
    sharpness = logit_scale[0]
    offset = bias[0]
    own_rows = images.shape[0]
    img_count = lax.axis_size("img")
    txt_count = lax.axis_size("txt")
    img_rows = own_rows * txt_count
    txt_rows = texts.shape[0]
    img_first = lax.axis_index("img") * img_rows
    txt_first = lax.axis_index("txt") * txt_rows
    own_text = texts.astype(jnp.float32)
    whole_text = lax.all_gather(texts, "img", axis=1, tiled=True).astype(jnp.float32)
    txt_norm = lax.rsqrt(jnp.sum(whole_text * whole_text, axis=1) + EPS)
    txt_unit = (whole_text * txt_norm[:, None]).astype(jnp.bfloat16)
    col_index = txt_first + jnp.arange(txt_rows, dtype=jnp.int32)
    whole_images = lax.all_gather(images, "txt", axis=0, tiled=True)
    piece_wide = whole_images.astype(jnp.float32)
    piece_norm = lax.rsqrt(jnp.sum(piece_wide * piece_wide, axis=1) + EPS)
    piece_unit = (piece_wide * piece_norm[:, None]).astype(jnp.bfloat16)
    logits = (
        sharpness
        * lax.dot_general(
            piece_unit, txt_unit, (((1,), (1,)), ((), ())), preferred_element_type=jnp.float32
        )
        + offset
    )
    row_index = img_first + jnp.arange(whole_images.shape[0], dtype=jnp.int32)
    labels = jnp.where(
        row_index[:, None] == col_index[None, :], jnp.float32(1.0), jnp.float32(-1.0)
    )
    loss_part = jnp.sum(jax.nn.softplus(-labels * logits))
    weights = (-labels * jax.nn.sigmoid(-labels * logits) * sharpness).astype(jnp.bfloat16)
    img_part = jnp.dot(weights, txt_unit, preferred_element_type=jnp.float32)
    txt_part = lax.dot_general(
        weights, piece_unit, (((0,), (0,)), ((), ())), preferred_element_type=jnp.float32
    )
    img_part, txt_part, loss_part = (img_part, txt_part, loss_part)
    d_img = lax.psum_scatter(
        img_part.astype(jnp.bfloat16), "txt", scatter_dimension=0, tiled=True
    ).astype(jnp.float32)
    d_txt = lax.psum_scatter(
        txt_part.astype(jnp.bfloat16), "img", scatter_dimension=1, tiled=True
    ).astype(jnp.float32)
    own_image = images.astype(jnp.float32)
    img_norm = lax.rsqrt(jnp.sum(own_image * own_image, axis=1) + EPS)
    img_inner = jnp.sum(own_image * d_img, axis=1)
    grad_images = (
        img_norm[:, None] * d_img
        - own_image * (img_norm * img_norm * img_norm * img_inner)[:, None]
    )
    txt_inner = lax.psum(jnp.sum(own_text * d_txt, axis=1), "img")
    grad_texts = (
        txt_norm[:, None] * d_txt - own_text * (txt_norm * txt_norm * txt_norm * txt_inner)[:, None]
    )
    total = lax.psum(loss_part, ("img", "txt"))
    loss = (total / (img_rows * img_count)).reshape(1)
    return (loss, grad_images, grad_texts)


def solution(mesh):
    return jax.shard_map(
        per_device,
        mesh=mesh,
        in_specs=(P(("img", "txt"), None), P("txt", "img"), P(), P()),
        out_specs=(P(), P(("img", "txt"), None), P("txt", "img")),
        check_vma=False,
    )
```

profile of v0, /device:TPU:34, one launch (start us, length us, event | category | flops | bytes accessed | tf_op | source)
XLA Modules:
  0.0 813.5 jit_solution(17910638645603441125)
XLA Ops:
  7.2 0.0 all-gather.3.cloned.1.call-start
  7.2 0.7 all-gather.3.cloned.1.call-update
  7.9 0.0 reduce-scatter.4.cloned.1.call-start
  9.3 65.8 %all_gather.7 = bf16[288,1152]{0,1:T(8,128)(2,1)S(1)} all-gather(bf16[288,72]{0,1:T(8,128)(2,1)} %param.5), channel_id=1, replica_groups=mesh['img'=16,'txt'=32] {'img'}, dimensions={1}, use_global_device_ids=true | all-gather | bytes 705024 | tf_op jit(solution)/shard_map/all_gather | solution.py:20
  75.0 0.3 fusion
  75.3 172.4 %all-gather.3.cloned.1.call-done = bf16[32,18,1152]{2,1,0:T(8,128)(2,1)} async-done(((bf16[1,18,1152]{2,1,0:T(8,128)(2,1)}), bf16[32,18,1152]{2,1,0:T(8,128)(2,1)}) %all-gather.3.cloned.1.call-update) | async-done | bytes 1327120 | tf_op jit(solution)/shard_map/all_gather | solution.py:24
  247.8 2.4 reshape.40
  250.1 0.3 multiply_reduce_fusion
  250.4 2.8 fusion.6
  253.2 3.3 convolution_convert_fusion.1
  256.5 0.0 reduce-scatter.4.cloned.1.call-update
  256.5 0.0 all-reduce.4.cloned.1.call-start
  256.6 0.0 copy-start.1
  256.6 0.0 copy-start
  256.6 3.4 convolution_convert_fusion
  260.0 0.0 all-reduce.4.cloned.1.call-update
  260.0 1.3 dynamic-slice
  262.0 106.9 %psum.14 = f32[]{:T(128)} all-reduce(f32[]{:T(128)} %get-tuple-element.7), channel_id=1, replica_groups=mesh['img'=16,'txt'=32] {'img','txt'}, use_global_device_ids=true, to_apply=%region_3.4 | all-reduce | flops 1 | bytes 8 | tf_op jit(solution)/shard_map/psum | solution.py:63
  369.5 0.0 reduce-scatter.4.cloned.1.call-done
  369.5 0.0 copy-done.1
  369.5 0.9 fusion.9
  370.4 63.2 %psum.15 = f32[288]{0:T(512)S(1)} all-reduce(f32[288]{0:T(512)S(1)} %fusion.9), channel_id=1, replica_groups=mesh['img'=16,'txt'=32] {'img'}, use_global_device_ids=true, to_apply=%region_9.10 | all-reduce | flops 288 | bytes 2304 | tf_op jit(solution)/shard_map/psum | solution.py:59
  433.6 1.5 fusion.8
  435.1 368.0 %all-reduce.4.cloned.1.call-done = bf16[576,1152]{1,0:T(8,128)(2,1)} async-done(((bf16[576,1152]{1,0:T(8,128)(2,1)}), bf16[576,1152]{1,0:T(8,128)(2,1)}) %all-reduce.4.cloned.1.call-update) | async-done | bytes 1327120
  803.2 0.0 copy-done
  803.2 1.0 fusion.10
  804.2 1.6 fusion.7
  (6 shorter events, 0.0 us)
Async XLA Ops:
  7.2 240.6 %all-gather.3.cloned.1.call-start = ((), (), s32[]{:S(2)}) async-start(), calls=%async_computation.1 | async-start | bytes 1824768 | tf_op jit(solution)/shard_map/all_gather | solution.py:24
  7.9 361.6 %reduce-scatter.4.cloned.1.call-start = ((), (), s32[]{:S(2)}) async-start(), calls=%async_computation.3 | async-start | bytes 940032
  256.5 546.6 %all-reduce.4.cloned.1.call-start = ((), (), s32[]{:S(2)}) async-start(), calls=%async_computation.2 | async-start | bytes 2654208
  256.6 113.0 %copy-start.1 = (bf16[288,72]{0,1:T(8,128)(2,1)S(1)}, bf16[288,72]{0,1:T(8,128)(2,1)}, u32[]{:S(2)}) copy-start(bf16[288,72]{0,1:T(8,128)(2,1)} %param.5) | copy-start | bytes 124420
  256.6 546.6 %copy-start = (bf16[18,1152]{1,0:T(8,128)(2,1)S(1)}, bf16[18,1152]{1,0:T(8,128)(2,1)}, u32[]{:S(2)}) copy-start(bf16[18,1152]{1,0:T(8,128)(2,1)} %param.4) | copy-start | bytes 124420
Sparse Core Ops, SparseCore 0:
  10.1 237.6 all-gather.2
  256.6 99.1 reduce-scatter.3
  358.8 444.3 all-reduce.3
where the time goes:
time: 814 us; the launch traced here: 813 us
  waiting for transfers between devices  541 us (66%)
  blocking collectives  236 us (29%)
  between operations  17.5 us (2%)
  matrix products  9.52 us (1%)
    unnamed x5, waiting for transfers between devices  369 us
    all_gather x1, waiting for transfers between devices, per_device(): whole_images = lax.all_gather(images, 'txt', axis=0, tiled=True)  172 us
    psum x1, blocking collectives, per_device(): total = lax.psum(loss_part, ('img', 'txt'))  107 us
    all_gather x1, blocking collectives, per_device(): lax.all_gather(texts, 'img', axis=1, tiled=True).astype(jnp.float32)  65.8 us
    psum x1, blocking collectives, per_device(): txt_inner = lax.psum(jnp.sum(own_text * d_txt, axis=1), 'img')  63.2 us
  transfers between devices with their start and end apart: 3, of which 2 were waited for; matrix products, arithmetic and copies ran while one was open for 1% of the time, Pallas kernels for 0%

commit v1 on v0

v1 whole, which is shorter than its diff:
```python
import functools

import jax
import jax.numpy as jnp
from jax import lax
from jax.experimental import pallas as pl
from jax.experimental.pallas import tpu as pltpu
from jax.sharding import PartitionSpec as P

EPS = 1e-06
F32 = jnp.float32
BF16 = jnp.bfloat16
MESH = pl.DeviceIdType.MESH
D = 1152
PAIRS = 9216
ROWS = 18
SLAB = 72
SLABP = 80
COLS = 72
TXT = 288
PIECE = 80


def dot(a, b, dims):
    return lax.dot_general(a, b, (dims, ((), ())), preferred_element_type=F32)


def pack(data, inner):
    high = inner.astype(BF16).astype(F32)
    low = inner - high
    row = lax.broadcasted_iota(jnp.int32, (8, TXT), 0)
    tail = jnp.where(row == 0, high, jnp.where(row == 1, low, 0.0))
    return jnp.concatenate([data, tail], axis=0).astype(BF16)


def unpack(piece):
    wide = piece.astype(F32)
    return wide[:COLS], wide[COLS : COLS + 1] + wide[COLS + 1 : COLS + 2]


def kernel(
    images, texts, scale, bias, loss_out, img_out, txt_out,
    xz, xf, xs, ts, tt, inv_txt, w1, iy_send, iy_recv, iown, iz_send, iz_recv,
    dtf, cs_send, cs_recv, tx_send, tx_recv, tx_own, tb_send, tb_recv, tb_own, th_send, th_recv,
    pad_a, pad_b, ls,
    xz_ss, xz_rs, xs_ss, xs_rs, ts_ss, ts_rs, iy_ss, iy_rs, iz_ss, iz_rs,
    cs_ss, cs_rs, tx_ss, tx_rs, tb_ss, tb_rs, th_ss, th_rs, ls_ss, ls_rs,
):
    i = lax.axis_index("img")
    t = lax.axis_index("txt")
    x, zh, c = i // 4, (i // 2) % 2, i % 2
    y, zm, zb = t // 8, (t // 2) % 4, t % 2
    zbp, zhp, cp = 1 - zb, 1 - zh, 1 - c

    def dev(x=x, zh=zh, c=c, y=y, zm=zm, zb=zb):
        return (x * 4 + zh * 2 + c, y * 8 + zm * 2 + zb)

    def turn(v, d):
        return lax.rem(v + d, 4)

    order = (1, 3, 2)
    peers = [dev(zh=zhp), dev(zb=zbp), dev(c=cp)]
    for d in order:
        peers += [dev(x=turn(x, d)), dev(y=turn(y, d)), dev(zm=turn(zm, d))]
    barrier = pltpu.get_barrier_semaphore()
    for peer in peers:
        pl.semaphore_signal(barrier, inc=1, device_id=peer, device_id_type=MESH)

    pending = []

    def copy(src, dst, ss, rs, peer):
        return pltpu.make_async_remote_copy(
            src_ref=src, dst_ref=dst, send_sem=ss, recv_sem=rs, device_id=peer, device_id_type=MESH
        )

    def send(*args):
        one = copy(*args)
        one.start()
        pending.append(one)

    sharpness = scale[0]
    offset = bias[0]

    pad_a[0:TXT, 0:COLS] = texts[...].astype(F32)
    ts[zb, x, zh, c] = pad_a[...].T[0:COLS, 0:TXT].astype(BF16)
    own_image = images[...].astype(F32)
    img_norm = lax.rsqrt(jnp.sum(own_image * own_image, axis=1, keepdims=True) + EPS)
    xz[zm] = (own_image * img_norm).astype(BF16)

    pl.semaphore_wait(barrier, len(peers))

    slots = [0]

    def t_send(b, xx, h, peer):
        k = slots[0]
        slots[0] += 1
        send(ts.at[b, xx, h, c], ts.at[b, xx, h, c], ts_ss.at[k], ts_rs.at[b, xx, h, c], peer)

    def t_wait(b, xx, h, cc):
        ref = ts.at[b, xx, h, cc]
        copy(ref, ref, ts_ss.at[0], ts_rs.at[b, xx, h, cc], dev(c=cp)).wait_recv()

    def to_x(b, h):
        for d in order:
            t_send(b, x, h, dev(x=turn(x, d)))

    def to_c(b, xx, h):
        t_send(b, xx, h, dev(c=cp))

    t_send(zb, x, zh, dev(zh=zhp))
    t_send(zb, x, zh, dev(zb=zbp))
    for k, d in enumerate((2, 1, 3)):
        send(xz.at[zm], xz.at[zm], xz_ss.at[k], xz_rs.at[zm], dev(zm=turn(zm, d)))
    to_x(zb, zh)
    to_c(zb, x, zh)
    t_wait(zbp, x, zh, c)
    to_x(zbp, zh)
    to_c(zbp, x, zh)

    for d in order:
        q = turn(zm, d)
        copy(xz.at[q], xz.at[q], xz_ss.at[0], xz_rs.at[q], dev(zm=q)).wait_recv()
    for q in range(4):
        xf[q * ROWS : (q + 1) * ROWS, :] = xz[q].astype(F32)
    xf[SLAB:SLABP, :] = jnp.zeros((SLABP - SLAB, D), F32)
    xs[y] = xf[...].astype(BF16)
    for k, d in enumerate((2, 1, 3)):
        send(xs.at[y], xs.at[y], xs_ss.at[k], xs_rs.at[y], dev(y=turn(y, d)))

    t_wait(zb, x, zhp, c)
    t_send(zb, x, zhp, dev(zb=zbp))
    to_x(zb, zhp)
    to_c(zb, x, zhp)
    t_wait(zbp, x, zhp, c)
    to_x(zbp, zhp)
    to_c(zbp, x, zhp)
    for b, h in ((zb, zh), (zbp, zh), (zb, zhp), (zbp, zhp)):
        for d in order:
            xx = turn(x, d)
            t_wait(b, xx, h, c)
            to_c(b, xx, h)
    for b, h in ((zb, zh), (zbp, zh), (zb, zhp), (zbp, zhp)):
        for d in (0, 1, 3, 2):
            t_wait(b, turn(x, d), h, cp)
    for b in range(2):
        square = jnp.zeros((8, TXT), F32)
        for j in range(8):
            both = jnp.concatenate(
                [ts[b, j // 2, j % 2, 0].astype(F32), ts[b, j // 2, j % 2, 1].astype(F32)], axis=0
            )
            tt[b, j * 144 : (j + 1) * 144, :] = both.astype(BF16)
            square += jnp.sum((both * both).reshape(18, 8, TXT), axis=0)
        inv_txt[b] = lax.rsqrt(jnp.sum(square, axis=0, keepdims=True) + EPS)

    row = lax.broadcasted_iota(jnp.int32, (SLABP, TXT), 0)
    col = lax.broadcasted_iota(jnp.int32, (SLABP, TXT), 1)
    gap = (row >= 18).astype(jnp.int32) + (row >= 36).astype(jnp.int32) + (row >= 54).astype(jnp.int32)
    row_in = row + 18 * gap - col + (i * 576 + zb * 18 - (y * 8 + zm * 2) * TXT)
    valid = row < SLAB
    loss_row = jnp.zeros((1, TXT), F32)
    inner = [jnp.zeros((1, TXT), F32) for _ in range(2)]
    for k, d in enumerate((0, 1, 3, 2)):
        yy = turn(y, d)
        if d:
            copy(xs.at[yy], xs.at[yy], xs_ss.at[0], xs_rs.at[yy], dev(y=yy)).wait_recv()
        slab = xs[yy]
        term = jnp.zeros((SLABP, D), F32)
        for b in range(2):
            raw = dot(slab, tt[b], ((1,), (0,)))
            logits = raw * (sharpness * inv_txt[b]) + offset
            diagonal = row_in == b * TXT - yy * 144
            sign = jnp.where(diagonal, -1.0, 1.0)
            u = sign * logits
            e = jnp.exp(-jnp.abs(u))
            soft = jnp.maximum(u, 0.0) + jnp.log1p(e)
            loss_row += jnp.sum(jnp.where(valid, soft, 0.0), axis=0, keepdims=True)
            w = sign * (jnp.where(u >= 0, 1.0, e) / (1.0 + e)) * sharpness
            w = jnp.where(valid, w, 0.0)
            wb = w.astype(BF16)
            inner[b] += jnp.sum(wb.astype(F32) * raw, axis=0, keepdims=True)
            w1[b, yy] = wb
            term += dot((w * inv_txt[b]).astype(BF16), tt[b], ((1,), (1,)))
        if d:
            iy_send[yy] = term.astype(BF16)
            send(iy_send.at[yy], iy_recv.at[y], iy_ss.at[k], iy_rs.at[y], dev(y=yy))
        else:
            iown[...] = term

    def loss_send(stage, place, others, value):
        ls[stage, place] = jnp.full((8, 128), value, F32)
        for k, peer in enumerate(others):
            send(ls.at[stage, place], ls.at[stage, place], ls_ss.at[stage, k], ls_rs.at[stage, place], peer)

    def loss_wait(stage, places, n):
        for q in places:
            copy(ls.at[stage, q], ls.at[stage, q], ls_ss.at[stage, 0], ls_rs.at[stage, q], dev(c=cp)).wait_recv()
        total = ls[stage, 0]
        for q in range(1, n):
            total += ls[stage, q]
        return total

    loss_send(0, c, [dev(c=cp)], jnp.sum(loss_row))

    for b in range(2):
        weights = w1[b].reshape(4 * SLABP, TXT)
        for q in range(3):
            part = xs[:, :, q * 384 : (q + 1) * 384].reshape(4 * SLABP, 384)
            dtf[b, q * 384 : (q + 1) * 384, :] = dot(part, weights, ((0,), (0,)))

    def features(b, xx, h, cc):
        return dtf[b, pl.ds(pl.multiple_of((xx * 4 + h * 2 + cc) * COLS, 8), COLS), :]

    for b in range(2):
        for xx in range(4):
            for h in range(2):
                cs_send[b, xx, h] = pack(features(b, xx, h, cp), inner[b])
                send(cs_send.at[b, xx, h], cs_recv.at[b, xx, h], cs_ss.at[b, xx, h], cs_rs.at[b, xx, h], dev(c=cp))

    loss_v = loss_wait(0, [cp], 2)
    loss_send(1, y, [dev(y=turn(y, d)) for d in order], loss_v)

    total = iown[...]
    for d in order:
        q = turn(y, d)
        copy(iy_recv.at[q], iy_recv.at[q], iy_ss.at[0], iy_rs.at[q], dev(y=q)).wait_recv()
        total += iy_recv[q].astype(F32)
    xf[...] = total
    for q in range(4):
        iz_send[q] = xf[q * ROWS : (q + 1) * ROWS, :].astype(BF16)
    for k, d in enumerate((2, 1, 3)):
        q = turn(zm, d)
        send(iz_send.at[q], iz_recv.at[zm], iz_ss.at[k], iz_rs.at[zm], dev(zm=q))
    loss_v = loss_wait(1, [turn(y, d) for d in order], 4)
    loss_send(2, zm, [dev(zm=turn(zm, d)) for d in order], loss_v)

    for d in (1, 3, 2, 0):
        xx = turn(x, d)
        for k, (b, h) in enumerate(((zbp, zhp), (zb, zhp), (zbp, zh), (zb, zh))):
            ref = cs_recv.at[b, xx, h]
            copy(ref, ref, cs_ss.at[0, 0, 0], cs_rs.at[b, xx, h], dev(c=cp)).wait_recv()
            data, inn = unpack(cs_recv[b, xx, h])
            own_inn = jnp.where(b == 0, inner[0], inner[1])
            data += features(b, xx, h, c)
            inn += own_inn
            if d:
                tx_send[xx, b, h] = pack(data, inn)
                send(tx_send.at[xx, b, h], tx_recv.at[x, b, h], tx_ss.at[d, k], tx_rs.at[x, b, h], dev(x=xx))
            else:
                tx_own[b, h, 0:COLS] = data
                tx_own[b, h, COLS:PIECE] = jnp.broadcast_to(inn, (8, TXT))

    q0 = iz_send[zm].astype(F32)
    for d in order:
        q = turn(zm, d)
        copy(iz_recv.at[q], iz_recv.at[q], iz_ss.at[0], iz_rs.at[q], dev(zm=q)).wait_recv()
        q0 += iz_recv[q].astype(F32)
    own_image = images[...].astype(F32)
    img_norm = lax.rsqrt(jnp.sum(own_image * own_image, axis=1, keepdims=True) + EPS)
    img_inner = jnp.sum(own_image * q0, axis=1, keepdims=True)
    img_out[...] = img_norm * q0 - own_image * (img_norm * img_norm * img_norm * img_inner)
    loss_v = loss_wait(2, [turn(zm, d) for d in order], 4)
    loss_send(3, x, [dev(x=turn(x, d)) for d in order], loss_v)

    def over_x(b, h):
        data = tx_own[b, h, 0:COLS]
        inn = tx_own[b, h, COLS : COLS + 1]
        for d in order:
            xx = turn(x, d)
            ref = tx_recv.at[xx, b, h]
            copy(ref, ref, tx_ss.at[1, 0], tx_rs.at[xx, b, h], dev(x=xx)).wait_recv()
            more, more_inn = unpack(tx_recv[xx, b, h])
            data += more
            inn += more_inn
        return data, inn

    for k, h in enumerate((zhp, zh)):
        tb_send[h] = pack(*over_x(zbp, h))
        send(tb_send.at[h], tb_recv.at[h], tb_ss.at[k], tb_rs.at[h], dev(zb=zbp))
    loss_v = loss_wait(3, [turn(x, d) for d in order], 4)
    loss_send(4, zb, [dev(zb=zbp)], loss_v)

    def over_pair(h):
        data, inn = over_x(zb, h)
        copy(tb_recv.at[h], tb_recv.at[h], tb_ss.at[0], tb_rs.at[h], dev(zb=zbp)).wait_recv()
        more, more_inn = unpack(tb_recv[h])
        return data + more, inn + more_inn

    th_send[...] = pack(*over_pair(zhp))
    send(th_send, th_recv, th_ss, th_rs, dev(zh=zhp))
    loss_v = loss_wait(4, [zbp], 2)
    loss_send(5, zh, [dev(zh=zhp)], loss_v)
    data, inn = over_pair(zh)
    copy(th_recv, th_recv, th_ss, th_rs, dev(zh=zhp)).wait_recv()
    more, more_inn = unpack(th_recv[...])
    data += more
    inn += more_inn
    norm = inv_txt[zb]
    grad = norm * data - ts[zb, x, zh, c].astype(F32) * (norm * norm * norm * inn)
    pad_b[0:COLS, 0:TXT] = grad
    txt_out[...] = pad_b[...].T[0:TXT, 0:COLS]
    loss_v = loss_wait(5, [zhp], 2)
    loss_out[0] = jnp.max(loss_v) / PAIRS
    for one in pending:
        one.wait_send()


def per_device(images, texts, logit_scale, bias):
    vmem = pl.BlockSpec(memory_space=pltpu.VMEM)
    smem = pl.BlockSpec(memory_space=pltpu.SMEM)
    sem = pltpu.SemaphoreType.DMA
    return pl.pallas_call(
        kernel,
        out_shape=(
            jax.ShapeDtypeStruct((1,), F32),
            jax.ShapeDtypeStruct((ROWS, D), F32),
            jax.ShapeDtypeStruct((TXT, COLS), F32),
        ),
        in_specs=[vmem, vmem, smem, smem],
        out_specs=(smem, vmem, vmem),
        scratch_shapes=[
            pltpu.VMEM((4, ROWS, D), BF16),
            pltpu.VMEM((SLABP, D), F32),
            pltpu.VMEM((4, SLABP, D), BF16),
            pltpu.VMEM((2, 4, 2, 2, COLS, TXT), BF16),
            pltpu.VMEM((2, D, TXT), BF16),
            pltpu.VMEM((2, 1, TXT), F32),
            pltpu.VMEM((2, 4, SLABP, TXT), BF16),
            pltpu.VMEM((4, SLABP, D), BF16),
            pltpu.VMEM((4, SLABP, D), BF16),
            pltpu.VMEM((SLABP, D), F32),
            pltpu.VMEM((4, ROWS, D), BF16),
            pltpu.VMEM((4, ROWS, D), BF16),
            pltpu.VMEM((2, D, TXT), F32),
            pltpu.VMEM((2, 4, 2, PIECE, TXT), BF16),
            pltpu.VMEM((2, 4, 2, PIECE, TXT), BF16),
            pltpu.VMEM((4, 2, 2, PIECE, TXT), BF16),
            pltpu.VMEM((4, 2, 2, PIECE, TXT), BF16),
            pltpu.VMEM((2, 2, PIECE, TXT), F32),
            pltpu.VMEM((2, PIECE, TXT), BF16),
            pltpu.VMEM((2, PIECE, TXT), BF16),
            pltpu.VMEM((2, PIECE, TXT), F32),
            pltpu.VMEM((PIECE, TXT), BF16),
            pltpu.VMEM((PIECE, TXT), BF16),
            pltpu.VMEM((384, 128), F32),
            pltpu.VMEM((128, 384), F32),
            pltpu.VMEM((6, 4, 8, 128), F32),
            sem((3,)), sem((4,)),
            sem((3,)), sem((4,)),
            sem((32,)), sem((2, 4, 2, 2)),
            sem((4,)), sem((4,)),
            sem((3,)), sem((4,)),
            sem((2, 4, 2)), sem((2, 4, 2)),
            sem((4, 4)), sem((4, 2, 2)),
            sem((2,)), sem((2,)),
            sem, sem,
            sem((6, 3)), sem((6, 4)),
        ],
        compiler_params=pltpu.CompilerParams(
            collective_id=0, has_side_effects=True, vmem_limit_bytes=48 * 1024 * 1024
        ),
        name="siglip",
    )(images, texts, logit_scale, bias)


def solution(mesh):
    return jax.shard_map(
        per_device,
        mesh=mesh,
        in_specs=(P(("img", "txt"), None), P("txt", "img"), P(), P()),
        out_specs=(P(), P(("img", "txt"), None), P("txt", "img")),
        check_vma=False,
    )
```

time: 814 us -> 89.7 us (0.11)
  the two profiles are of different devices: /device:TPU:34 before, /device:TPU:40 now
where the time goes in v1:
time: 89.7 us; the launch traced here: 89.5 us
  Pallas kernels  83.4 us (93%)
  between operations  3.72 us (4%)
  local copies, waits for them, and re-layouts  2.36 us (3%)
    pallas_call x1, Pallas kernels, per_device(): pl.pallas_call(kernel, out_shape=(jax.ShapeDtypeStruct((1,), F32), jax.Sh...  83.4 us

profile of v1, /device:TPU:40, one launch (start us, length us, event | category | flops | bytes accessed | tf_op | source)
XLA Modules:
  0.0 89.5 jit_solution(12799667807645093878)
XLA Ops:
  1.9 0.0 copy-start
  1.9 0.9 %copy.7.texts = bf16[288,72]{1,0:T(8,128)(2,1)S(1)} copy(bf16[288,72]{0,1:T(8,128)(2,1)} %param.5) | data formatting | bytes 82944 | tf_op args[1]
  2.9 0.0 copy-done
  2.9 83.4 %siglip.1 = (f32[1]{0:T(128)}, f32[18,1152]{1,0:T(8,128)S(1)}, f32[288,72]{1,0:T(8,128)S(1)}) custom-call(bf16[18,1152]{1,0:T(8,128)(2,1)S(1)} %copy-done, bf16[288,72]{1,0:T(8,128)(2,1)S(1)} %copy.7.texts, f32[1]{0:T(128)S(6)} %copy.11.scale, f32[1]{0:T(128)S(6)} %copy.12.bias), custom_call_target="tpu_custom_call" | custom-call | tf_op jit(solution)/shard_map/siglip/pallas_call | solution.py:311
  86.3 0.8 copy.8
  87.7 0.6 copy.14
Async XLA Ops:
  1.9 1.0 %copy-start = (bf16[18,1152]{1,0:T(8,128)(2,1)S(1)}, bf16[18,1152]{1,0:T(8,128)(2,1)}, u32[]{:S(2)}) copy-start(bf16[18,1152]{1,0:T(8,128)(2,1)} %images.1) | copy-start | bytes 124420

commit v2 on v0

v2 whole, which is shorter than its diff:
```python
import jax
import jax.numpy as jnp
from jax import lax
from jax.experimental import pallas as pl
from jax.experimental.pallas import tpu as pltpu
from jax.sharding import PartitionSpec as P

EPS = 1e-06
F32 = jnp.float32
BF16 = jnp.bfloat16
MESH = pl.DeviceIdType.MESH
D = 1152
PAIRS = 9216
ROWS = 18
HALF = 72
SLAB = 144
COLS = 72
TXT = 288
PIECE = 80


def dot(a, b, dims):
    return lax.dot_general(a, b, (dims, ((), ())), preferred_element_type=F32)


def pack(data, inner):
    high = inner.astype(BF16).astype(F32)
    low = inner - high
    row = lax.broadcasted_iota(jnp.int32, (8, TXT), 0)
    tail = jnp.where(row == 0, high, jnp.where(row == 1, low, 0.0))
    return jnp.concatenate([data, tail], axis=0).astype(BF16)


def unpack(piece):
    wide = piece.astype(F32)
    return wide[:COLS], wide[COLS : COLS + 1] + wide[COLS + 1 : COLS + 2]


def kernel(
    images, texts, scale, bias, loss_out, img_out, txt_out,
    xz, xf, xs, ts, tt, inv_own, inv_far, w1, term, iown, ic_send, ic_recv, iy_send, iy_recv, iz_send, iz_recv,
    dtf, tx_send, tx_recv, tacc, tb_send, tb_recv, tf_send, tf_recv, fin, ls,
    xz_ss, xz_rs, xc_ss, xc_rs, ts_ss, ts_rs, inv_ss, inv_rs, ic_ss, ic_rs, iy_ss, iy_rs, iz_ss, iz_rs,
    tx_ss, tx_rs, tb_ss, tb_rs, tf_ss, tf_rs, ls_ss, ls_rs,
):
    i = lax.axis_index("img")
    t = lax.axis_index("txt")
    x, zh, c = i // 4, (i // 2) % 2, i % 2
    y, zm, zb = t // 8, (t // 2) % 4, t % 2
    zbp, zhp, cp = 1 - zb, 1 - zh, 1 - c
    is_home = c == zb
    is_guest = c != zb

    def dev(x=x, zh=zh, c=c, y=y, zm=zm, zb=zb):
        return (x * 4 + zh * 2 + c, y * 8 + zm * 2 + zb)

    def turn(v, d):
        return lax.rem(v + d, 4)

    near = zm + 1 - 2 * (zm % 2)
    far = turn(zm, 2)
    last = turn(near, 2)
    order = (1, 3, 2)
    peers = [dev(c=cp)]
    for cc in range(2):
        peers += [dev(zh=zhp, c=cc), dev(zb=zbp, c=cc)]
    for d in order:
        peers += [dev(x=turn(x, d)), dev(y=turn(y, d)), dev(zm=turn(zm, d))]
    barrier = pltpu.get_barrier_semaphore()
    for peer in peers:
        pl.semaphore_signal(barrier, inc=1, device_id=peer, device_id_type=MESH)

    pending = {"all": [], "home": [], "guest": []}

    def copy(src, dst, ss, rs, peer):
        return pltpu.make_async_remote_copy(
            src_ref=src, dst_ref=dst, send_sem=ss, recv_sem=rs, device_id=peer, device_id_type=MESH
        )

    def send(src, dst, ss, rs, peer, who="all", like=None):
        copy(src, dst, ss[0].at[ss[1:]] if ss[1:] else ss[0], rs, peer).start()
        pending[who].append((like or (lambda: src), ss))

    def sent(who):
        for like, ss in pending[who]:
            ref = like()
            copy(ref, ref, ss[0].at[ss[1:]] if ss[1:] else ss[0], ls_rs.at[0, 0], dev(c=cp)).wait_send()

    def arrived(ref, rs):
        copy(ref, ref, ls_ss.at[0, 0], rs, dev(c=cp)).wait_recv()

    sharpness = scale[0]
    offset = bias[0]

    own_image = images[...].astype(F32)
    img_norm = lax.rsqrt(jnp.sum(own_image * own_image, axis=1, keepdims=True) + EPS)
    xz[y, c, zm] = (own_image * img_norm).astype(BF16)

    pl.semaphore_wait(barrier, len(peers))

    counts = {"home": 0, "guest": 0}

    def t_send(who, xx, h, cc, peer, own=False):
        k = counts[who]
        counts[who] += 1
        slot = ts.at[xx, h, cc]
        send(texts if own else slot, slot, (ts_ss, k), ts_rs.at[xx, h, cc], peer, who, lambda: texts)

    def t_wait(xx, h, cc):
        arrived(ts.at[xx, h, cc], ts_rs.at[xx, h, cc])

    def t_over_x(who, h, cc, own=False):
        for d in (2, 1, 3):
            t_send(who, x, h, cc, dev(x=turn(x, d)), own)

    x_count = [0]

    def x_send(q, peer):
        k = x_count[0]
        x_count[0] += 1
        slot = xz.at[y, c, q]
        send(slot, slot, (xz_ss, k), xz_rs.at[y, q], peer)

    def x_wait(yy, q):
        arrived(xz.at[yy, c, q], xz_rs.at[yy, q])

    def x_over_y(q):
        for d in (2, 1, 3):
            x_send(q, dev(y=turn(y, d)))

    def x_to_core(k, yy):
        group = xz.at[yy, c]
        send(group, group, (xc_ss, k), xc_rs.at[yy], dev(c=cp))

    @pl.when(is_home)
    def _():
        t_send("home", x, zh, c, dev(zh=zhp), True)
        t_send("home", x, zh, c, dev(zb=zbp), True)
        t_over_x("home", zh, c, True)
        ts[x, zh, c] = texts[...]

    @pl.when(is_guest)
    def _():
        t_send("guest", x, zh, c, dev(zh=zhp, c=cp), True)
        t_send("guest", x, zh, c, dev(zb=zbp, c=cp), True)
        t_send("guest", x, zh, c, dev(c=cp), True)

    x_send(zm, dev(zm=far))
    x_send(zm, dev(zm=near))
    x_over_y(zm)

    @pl.when(is_home)
    def _():
        t_wait(x, zh, cp)
        t_over_x("home", zh, cp)

    @pl.when(is_guest)
    def _():
        for cc in range(2):
            t_wait(x, zh, cc)
            t_over_x("guest", zh, cc)

    x_wait(y, near)
    x_over_y(near)
    x_wait(y, far)
    x_send(far, dev(zm=near))
    x_over_y(far)

    @pl.when(is_home)
    def _():
        for cc in range(2):
            t_wait(x, zhp, cc)
            t_send("home", x, zhp, cc, dev(zb=zbp))
            t_over_x("home", zhp, cc)

    x_wait(y, last)
    x_over_y(last)
    x_to_core(0, y)

    @pl.when(is_guest)
    def _():
        for cc in range(2):
            t_wait(x, zhp, cc)
            t_over_x("guest", zhp, cc)

    for d in order:
        yy = turn(y, d)
        for q in range(4):
            x_wait(yy, turn(zm, q))
        x_to_core(d, yy)
    for h in (zh, zhp):
        for cc in range(2):
            for d in order:
                t_wait(turn(x, d), h, cc)

    square = jnp.zeros((8, TXT), F32)
    for j in range(8):
        both = jnp.concatenate([ts[j // 2, j % 2, 0].astype(F32), ts[j // 2, j % 2, 1].astype(F32)], axis=0)
        tt[j * 144 : (j + 1) * 144, :] = both.astype(BF16)
        square += jnp.sum((both * both).reshape(18, 8, TXT), axis=0)
    inv_txt = lax.rsqrt(jnp.sum(square, axis=0, keepdims=True) + EPS)
    inv_own[...] = jnp.broadcast_to(inv_txt, (8, TXT))

    @pl.when(is_home)
    def _():
        send(inv_own, inv_far, (inv_ss,), inv_rs, dev(c=cp), "home")

    row = lax.broadcasted_iota(jnp.int32, (SLAB, TXT), 0)
    col = lax.broadcasted_iota(jnp.int32, (SLAB, TXT), 1)
    side = (row >= HALF).astype(jnp.int32)
    rest = row - HALF * side
    gap = (rest >= 18).astype(jnp.int32) + (rest >= 36).astype(jnp.int32) + (rest >= 54).astype(jnp.int32)
    ahead = row + 504 * side + 18 * gap - col
    ahead += (x * 4 + zh * 2) * 576 + zb * 18 - (y * 8 + zm * 2 + c) * TXT
    loss_row = jnp.zeros((1, TXT), F32)
    inner = jnp.zeros((1, TXT), F32)

    def from_core(k, yy):
        arrived(ic_recv.at[yy], ic_rs.at[yy])
        total = iown[yy] + ic_recv[yy].astype(F32)
        if k < 3:
            iy_send[yy] = total.astype(BF16)
            send(iy_send.at[yy], iy_recv.at[y], (iy_ss, k), iy_rs.at[y], dev(y=yy))
        return total

    before = None
    for k, d in enumerate((2, 1, 3, 0)):
        yy = turn(y, d)
        arrived(xz.at[yy, cp], xc_rs.at[yy])
        for side_of in range(2):
            for q in range(4):
                first = side_of * HALF + q * ROWS
                xf[first : first + ROWS, :] = xz[yy, side_of, q].astype(F32)
        xs[yy] = xf[...].astype(BF16)
        slab = xs[yy]
        raw = dot(slab, tt[...], ((1,), (0,)))
        logits = raw * (sharpness * inv_txt) + offset
        diagonal = ahead == -144 * yy
        sign = jnp.where(diagonal, -1.0, 1.0)
        u = sign * logits
        e = jnp.exp(-jnp.abs(u))
        loss_row += jnp.sum(jnp.maximum(u, 0.0) + jnp.log1p(e), axis=0, keepdims=True)
        w = sign * (jnp.where(u >= 0, 1.0, e) / (1.0 + e)) * sharpness
        wb = w.astype(BF16)
        inner += jnp.sum(wb.astype(F32) * raw, axis=0, keepdims=True)
        w1[yy] = wb
        term[...] = dot((w * inv_txt).astype(BF16), tt[...], ((1,), (1,)))
        ic_send[yy] = term[pl.ds(pl.multiple_of(cp * HALF, 8), HALF), :].astype(BF16)
        send(ic_send.at[yy], ic_recv.at[yy], (ic_ss, k), ic_rs.at[yy], dev(c=cp))
        iown[yy] = term[pl.ds(pl.multiple_of(c * HALF, 8), HALF), :]
        if before is not None:
            from_core(*before)
        before = (k, yy)

    def loss_send(stage, place, others, value):
        ls[stage, place] = jnp.full((8, 128), value, F32)
        for k, peer in enumerate(others):
            send(ls.at[stage, place], ls.at[stage, place], (ls_ss, stage, k), ls_rs.at[stage, place], peer)

    def loss_wait(stage, places, n):
        for q in places:
            arrived(ls.at[stage, q], ls_rs.at[stage, q])
        total = ls[stage, 0]
        for q in range(1, n):
            total += ls[stage, q]
        return total

    loss_send(0, c, [dev(c=cp)], jnp.sum(loss_row))

    weights = w1[...].reshape(4 * SLAB, TXT)
    for q in range(3):
        part = xs[:, :, q * 384 : (q + 1) * 384].reshape(4 * SLAB, 384)
        dtf[q * 384 : (q + 1) * 384, :] = dot(part, weights, ((0,), (0,)))

    def features(xx, h, cc):
        return dtf[pl.ds(pl.multiple_of((xx * 4 + h * 2 + cc) * COLS, 8), COLS), :]

    for j, h in enumerate((zhp, zh)):
        for d in (2, 1, 3):
            xx = turn(x, d)
            for cc in range(2):
                tx_send[xx, h, cc] = pack(features(xx, h, cc), inner)
            send(tx_send.at[xx, h], tx_recv.at[x, h], (tx_ss, j, d - 1), tx_rs.at[x, h], dev(x=xx))

    total = from_core(*before)
    loss_v = loss_wait(0, [cp], 2)
    loss_send(1, y, [dev(y=turn(y, d)) for d in order], loss_v)
    for d in order:
        q = turn(y, d)
        arrived(iy_recv.at[q], iy_rs.at[q])
        total += iy_recv[q].astype(F32)
    xf[0:HALF, :] = total
    for q in range(4):
        iz_send[q] = xf[q * ROWS : (q + 1) * ROWS, :].astype(BF16)
    for k, d in enumerate((2, 1, 3)):
        q = turn(zm, d)
        send(iz_send.at[q], iz_recv.at[zm], (iz_ss, k), iz_rs.at[zm], dev(zm=q))
    loss_v = loss_wait(1, [turn(y, d) for d in order], 4)
    loss_send(2, zm, [dev(zm=turn(zm, d)) for d in order], loss_v)

    for j, h in enumerate((zhp, zh)):
        sums = [features(x, h, cc) for cc in range(2)]
        inn = inner
        for d in order:
            xx = turn(x, d)
            arrived(tx_recv.at[xx, h], tx_rs.at[xx, h])
            for cc in range(2):
                more, more_inn = unpack(tx_recv[xx, h, cc])
                sums[cc] += more
            inn += more_inn
        for cc in range(2):
            tacc[h, cc, 0:COLS] = sums[cc]
            tacc[h, cc, COLS:PIECE] = jnp.broadcast_to(inn, (8, TXT))

        @pl.when(is_guest)
        def _():
            for cc in range(2):
                tb_send[h, cc] = pack(tacc[h, cc, 0:COLS], tacc[h, cc, COLS : COLS + 1])
            send(tb_send.at[h], tb_recv.at[h], (tb_ss, j), tb_rs.at[h], dev(zb=zbp), "guest", lambda: tb_send.at[0])

    loss_v = loss_wait(2, [turn(zm, d) for d in order], 4)
    loss_send(3, x, [dev(x=turn(x, d)) for d in order], loss_v)

    @pl.when(is_home)
    def _():
        for h in (zhp, zh):
            arrived(tb_recv.at[h], tb_rs.at[h])
            for cc in range(2):
                more, more_inn = unpack(tb_recv[h, cc])
                data = tacc[h, cc, 0:COLS] + more
                inn = tacc[h, cc, COLS : COLS + 1] + more_inn
                tacc[h, cc, 0:COLS] = data
                tacc[h, cc, COLS:PIECE] = jnp.broadcast_to(inn, (8, TXT))
                if h is zhp:
                    tf_send[cc] = pack(data, inn)
                    send(tf_send.at[cc], tf_recv.at[1], (tf_ss, cc), tf_rs.at[1], dev(zh=zhp, c=cc), "home", lambda: tf_send.at[0])
        tf_send[2] = pack(tacc[zh, cp, 0:COLS], tacc[zh, cp, COLS : COLS + 1])
        send(tf_send.at[2], tf_recv.at[0], (tf_ss, 2), tf_rs.at[0], dev(c=cp), "home", lambda: tf_send.at[0])
        fin[...] = tacc[zh, c]

    loss_v = loss_wait(3, [turn(x, d) for d in order], 4)
    loss_send(4, zb, [dev(zb=zbp)], loss_v)

    total = iz_send[zm].astype(F32)
    for d in order:
        q = turn(zm, d)
        arrived(iz_recv.at[q], iz_rs.at[q])
        total += iz_recv[q].astype(F32)
    own_image = images[...].astype(F32)
    img_norm = lax.rsqrt(jnp.sum(own_image * own_image, axis=1, keepdims=True) + EPS)
    img_inner = jnp.sum(own_image * total, axis=1, keepdims=True)
    img_out[...] = img_norm * total - own_image * (img_norm * img_norm * img_norm * img_inner)
    loss_v = loss_wait(4, [zbp], 2)
    loss_send(5, zh, [dev(zh=zhp)], loss_v)

    @pl.when(is_guest)
    def _():
        arrived(inv_far, inv_rs)
        inv_own[...] = inv_far[...]
        arrived(tf_recv.at[0], tf_rs.at[0])
        data, inn = unpack(tf_recv[0])
        fin[0:COLS] = data
        fin[COLS:PIECE] = jnp.broadcast_to(inn, (8, TXT))

    arrived(tf_recv.at[1], tf_rs.at[1])
    more, more_inn = unpack(tf_recv[1])
    data = fin[0:COLS] + more
    inn = fin[COLS : COLS + 1] + more_inn
    norm = inv_own[0:1]
    txt_out[...] = norm * data - texts[...].astype(F32) * (norm * norm * norm * inn)
    loss_v = loss_wait(5, [zhp], 2)
    loss_out[0] = jnp.max(loss_v) / PAIRS

    sent("all")

    @pl.when(is_home)
    def _():
        sent("home")

    @pl.when(is_guest)
    def _():
        sent("guest")


def per_device(images, texts, logit_scale, bias):
    vmem = pl.BlockSpec(memory_space=pltpu.VMEM)
    smem = pl.BlockSpec(memory_space=pltpu.SMEM)
    sem = pltpu.SemaphoreType.DMA
    loss, grad_images, grad_texts = pl.pallas_call(
        kernel,
        out_shape=(
            jax.ShapeDtypeStruct((1,), F32),
            jax.ShapeDtypeStruct((ROWS, D), F32),
            jax.ShapeDtypeStruct((COLS, TXT), F32),
        ),
        in_specs=[vmem, vmem, smem, smem],
        out_specs=(smem, vmem, vmem),
        scratch_shapes=[
            pltpu.VMEM((4, 2, 4, ROWS, D), BF16),
            pltpu.VMEM((SLAB, D), F32),
            pltpu.VMEM((4, SLAB, D), BF16),
            pltpu.VMEM((4, 2, 2, COLS, TXT), BF16),
            pltpu.VMEM((D, TXT), BF16),
            pltpu.VMEM((8, TXT), F32),
            pltpu.VMEM((8, TXT), F32),
            pltpu.VMEM((4, SLAB, TXT), BF16),
            pltpu.VMEM((SLAB, D), F32),
            pltpu.VMEM((4, HALF, D), F32),
            pltpu.VMEM((4, HALF, D), BF16),
            pltpu.VMEM((4, HALF, D), BF16),
            pltpu.VMEM((4, HALF, D), BF16),
            pltpu.VMEM((4, HALF, D), BF16),
            pltpu.VMEM((4, ROWS, D), BF16),
            pltpu.VMEM((4, ROWS, D), BF16),
            pltpu.VMEM((D, TXT), F32),
            pltpu.VMEM((4, 2, 2, PIECE, TXT), BF16),
            pltpu.VMEM((4, 2, 2, PIECE, TXT), BF16),
            pltpu.VMEM((2, 2, PIECE, TXT), F32),
            pltpu.VMEM((2, 2, PIECE, TXT), BF16),
            pltpu.VMEM((2, 2, PIECE, TXT), BF16),
            pltpu.VMEM((3, PIECE, TXT), BF16),
            pltpu.VMEM((2, PIECE, TXT), BF16),
            pltpu.VMEM((PIECE, TXT), F32),
            pltpu.VMEM((6, 4, 8, 128), F32),
            sem((15,)), sem((4, 4)),
            sem((4,)), sem((4,)),
            sem((16,)), sem((4, 2, 2)),
            sem, sem,
            sem((4,)), sem((4,)),
            sem((3,)), sem((4,)),
            sem((3,)), sem((4,)),
            sem((2, 3)), sem((4, 2)),
            sem((2,)), sem((2,)),
            sem((3,)), sem((2,)),
            sem((6, 3)), sem((6, 4)),
        ],
        compiler_params=pltpu.CompilerParams(
            collective_id=0, has_side_effects=True, vmem_limit_bytes=48 * 1024 * 1024
        ),
        name="siglip",
    )(images, texts.T, logit_scale, bias)
    return loss, grad_images, grad_texts.T


def solution(mesh):
    return jax.shard_map(
        per_device,
        mesh=mesh,
        in_specs=(P(("img", "txt"), None), P("txt", "img"), P(), P()),
        out_specs=(P(), P(("img", "txt"), None), P("txt", "img")),
        check_vma=False,
    )
```

time: 814 us -> 85.5 us (0.11)
  the two profiles are of different devices: /device:TPU:34 before, /device:TPU:32 now
where the time goes in v2:
time: 85.5 us; the launch traced here: 85.2 us
  Pallas kernels  78.6 us (92%)
  between operations  3.7 us (4%)
  local copies, waits for them, and re-layouts  2.91 us (3%)
    pallas_call x1, Pallas kernels, per_device(): pl.pallas_call(kernel, out_shape=(jax.ShapeDtypeStruct((1,), F32), jax.Sh...  78.6 us
    unnamed x6, local copies, waits for them, and re-layouts  2.91 us

profile of v2, /device:TPU:32, one launch (start us, length us, event | category | flops | bytes accessed | tf_op | source)
XLA Modules:
  0.0 85.2 jit_solution(15021691459964368199)
XLA Ops:
  1.9 0.0 copy-start
  1.9 0.8 copy-done
  2.7 0.0 copy-start.1
  2.7 0.8 copy-done.1
  3.6 78.6 %siglip.1 = (f32[1]{0:T(128)}, f32[18,1152]{1,0:T(8,128)S(1)}, f32[72,288]{1,0:T(8,128)S(1)}) custom-call(bf16[18,1152]{1,0:T(8,128)(2,1)S(1)} %copy-done, bf16[72,288]{1,0:T(8,128)(2,1)S(1)} %bitcast.3, f32[1]{0:T(128)S(6)} %copy.10.scale, f32[1]{0:T(128)S(6)} %copy.11.bias), custom_call_target="tpu_custom_call" | custom-call | tf_op jit(solution)/shard_map/siglip/pallas_call | solution.py:389
  82.8 0.6 copy.13
  83.5 0.6 copy.14
Async XLA Ops:
  1.9 0.8 copy-start
  2.7 0.8 copy-start.1

commit v3 on v2

v3 whole, which is shorter than its diff:
```python
import jax
import jax.numpy as jnp
from jax import lax
from jax.experimental import pallas as pl
from jax.experimental.pallas import tpu as pltpu
from jax.sharding import PartitionSpec as P

EPS = 1e-06
F32 = jnp.float32
BF16 = jnp.bfloat16
MESH = pl.DeviceIdType.MESH
D = 1152
PAIRS = 9216
ROWS = 18
HALF = 72
SLAB = 144
COLS = 72
TXT = 288
LANES = 384
DENSE = 168
PIECE = 176


def dot(a, b, dims):
    return lax.dot_general(a, b, (dims, ((), ())), preferred_element_type=F32)


def pack(data, inner):
    row = lax.broadcasted_iota(jnp.int32, (8, 128), 0)
    high = inner.astype(BF16).astype(F32)
    low = pltpu.roll(inner - high, 3, 0)
    tail = jnp.where(row < 3, high, jnp.where(row < 6, low, 0.0))
    return jnp.concatenate([data, tail], axis=0).astype(BF16)


def unpack(piece):
    wide = piece.astype(F32)
    tail = wide[DENSE:PIECE]
    return wide[:DENSE], tail + pltpu.roll(tail, 5, 0)


def densify(tiles):
    last = tiles[2]
    rest = last[0:24] + pltpu.roll(last[24:48], 32, 1) + pltpu.roll(last[48:72], 64, 1)
    return jnp.concatenate([tiles[0], tiles[1], rest], axis=0)


def last_tile(rest):
    lane = lax.broadcasted_iota(jnp.int32, (24, 128), 1)
    parts = [rest, pltpu.roll(rest, 96, 1), pltpu.roll(rest, 64, 1)]
    return jnp.concatenate([jnp.where(lane < 32, part, 0.0) for part in parts], axis=0)


def kernel(
    images, texts, scale, bias, loss_out, img_out, txt_out,
    xz, xf, xs, tp, tpad, ts, tt, inv_own, inv_far, w1, term, iown, ic_send, ic_recv, iy_send, iy_recv, iz_send, iz_recv,
    dtf, tx_send, tx_recv, tf_send, tf_recv, fin, ls,
    xz_ss, xz_rs, xc_ss, xc_rs, ts_ss, ts_rs, inv_ss, inv_rs, ic_ss, ic_rs, iy_ss, iy_rs, iz_ss, iz_rs,
    tx_ss, tx_rs, tf_ss, tf_rs, ls_ss, ls_rs,
):
    i = lax.axis_index("img")
    t = lax.axis_index("txt")
    x, zh, c = i // 4, (i // 2) % 2, i % 2
    y, zb, zm = t // 8, (t // 4) % 2, t % 4
    zbp, zhp, cp = 1 - zb, 1 - zh, 1 - c
    is_home = c == zb
    is_guest = c != zb

    def dev(x=x, zh=zh, c=c, y=y, zm=zm, zb=zb):
        return (x * 4 + zh * 2 + c, y * 8 + zb * 4 + zm)

    def turn(v, d):
        return lax.rem(v + d, 4)

    order = (1, 3, 2)
    peers = [dev(c=cp)]
    for cc in range(2):
        peers += [dev(zh=zhp, c=cc), dev(zb=zbp, c=cc), dev(zh=zhp, zb=zbp, c=cc)]
    for d in order:
        peers += [dev(x=turn(x, d)), dev(y=turn(y, d)), dev(zm=turn(zm, d))]
    barrier = pltpu.get_barrier_semaphore()
    for peer in peers:
        pl.semaphore_signal(barrier, inc=1, device_id=peer, device_id_type=MESH)

    pending = {"all": [], "home": [], "guest": []}

    def copy(src, dst, ss, rs, peer):
        return pltpu.make_async_remote_copy(
            src_ref=src, dst_ref=dst, send_sem=ss, recv_sem=rs, device_id=peer, device_id_type=MESH
        )

    def send(src, dst, ss, rs, peer, who="all", like=None):
        copy(src, dst, ss[0].at[ss[1:]] if ss[1:] else ss[0], rs, peer).start()
        pending[who].append((like or (lambda: src), ss))

    def sent(who):
        for like, ss in pending[who]:
            ref = like()
            copy(ref, ref, ss[0].at[ss[1:]] if ss[1:] else ss[0], ls_rs.at[0, 0], dev(c=cp)).wait_send()

    def arrived(ref, rs):
        copy(ref, ref, ls_ss.at[0, 0], rs, dev(c=cp)).wait_recv()

    sharpness = scale[0]
    offset = bias[0]

    own_image = images[...].astype(F32)
    img_norm = lax.rsqrt(jnp.sum(own_image * own_image, axis=1, keepdims=True) + EPS)
    xz[y, c, zm] = (own_image * img_norm).astype(BF16)
    tpad[...] = jnp.zeros((COLS, LANES), F32)
    tpad[:, 0:TXT] = texts[...].astype(F32)
    tp[...] = densify([tpad[:, j * 128 : (j + 1) * 128] for j in range(3)]).astype(BF16)

    pl.semaphore_wait(barrier, len(peers))

    counts = {"home": 0, "guest": 0}

    def t_send(who, xx, h, cc, peer, own=False):
        k = counts[who]
        counts[who] += 1
        slot = ts.at[xx, h, cc]
        send(tp if own else slot, slot, (ts_ss, k), ts_rs.at[xx, h, cc], peer, who, lambda: tp)

    def t_wait(xx, h, cc):
        arrived(ts.at[xx, h, cc], ts_rs.at[xx, h, cc])

    def t_over_x(who, h, cc, own=False):
        for d in (2, 1, 3):
            t_send(who, x, h, cc, dev(x=turn(x, d)), own)

    x_count = [0]

    def x_send(q, peer):
        k = x_count[0]
        x_count[0] += 1
        slot = xz.at[y, c, q]
        send(slot, slot, (xz_ss, k), xz_rs.at[y, q], peer)

    def x_wait(yy, q):
        arrived(xz.at[yy, c, q], xz_rs.at[yy, q])

    def x_over_y(q):
        for d in (2, 1, 3):
            x_send(q, dev(y=turn(y, d)))

    def x_to_core(k, yy):
        group = xz.at[yy, c]
        send(group, group, (xc_ss, k), xc_rs.at[yy], dev(c=cp))

    @pl.when(is_home)
    def _():
        t_send("home", x, zh, c, dev(zb=zbp), True)
        t_send("home", x, zh, c, dev(zh=zhp, zb=zbp), True)
        t_over_x("home", zh, c, True)
        ts[x, zh, c] = tp[...]

    @pl.when(is_guest)
    def _():
        t_send("guest", x, zh, c, dev(zb=zbp, c=cp), True)
        t_send("guest", x, zh, c, dev(zh=zhp, zb=zbp, c=cp), True)
        t_send("guest", x, zh, c, dev(c=cp), True)

    for d in (1, 3, 2):
        x_send(zm, dev(zm=turn(zm, d)))
    x_over_y(zm)

    @pl.when(is_home)
    def _():
        t_wait(x, zh, cp)
        t_over_x("home", zh, cp)

    @pl.when(is_guest)
    def _():
        for h in (zh, zhp):
            t_wait(x, h, zh)
            t_send("guest", x, h, zh, dev(zh=1 - h, zb=zbp))
            t_over_x("guest", h, zh)

    for d in order:
        x_wait(y, turn(zm, d))
        x_over_y(turn(zm, d))
    x_to_core(0, y)

    @pl.when(is_guest)
    def _():
        for h in (zh, zhp):
            t_wait(x, h, zhp)
            t_over_x("guest", h, zhp)

    @pl.when(is_home)
    def _():
        for cc in range(2):
            t_wait(x, zhp, cc)
            t_over_x("home", zhp, cc)

    for d in order:
        yy = turn(y, d)
        for q in range(4):
            x_wait(yy, turn(zm, q))
        x_to_core(d, yy)
    for h in (zh, zhp):
        for cc in range(2):
            for d in order:
                t_wait(turn(x, d), h, cc)

    square = jnp.zeros((8, LANES), F32)
    for j in range(8):
        halves = []
        for cc in range(2):
            block = ts[j // 2, j % 2, cc].astype(F32)
            halves.append(jnp.concatenate([block[0:72], block[72:144], last_tile(block[144:DENSE])], axis=1))
        both = jnp.concatenate(halves, axis=0)
        tt[j * 144 : (j + 1) * 144, :] = both.astype(BF16)
        square += jnp.sum((both * both).reshape(18, 8, LANES), axis=0)
    inv_txt = lax.rsqrt(jnp.sum(square, axis=0, keepdims=True) + EPS)
    inv_own[...] = jnp.broadcast_to(inv_txt, (8, LANES))

    @pl.when(is_home)
    def _():
        send(inv_own, inv_far, (inv_ss,), inv_rs, dev(c=cp), "home")

    row = lax.broadcasted_iota(jnp.int32, (SLAB, LANES), 0)
    col = lax.broadcasted_iota(jnp.int32, (SLAB, LANES), 1)
    side = (row >= HALF).astype(jnp.int32)
    ahead = row + 504 * side - col + (x * 4 + zh * 2) * 576 + zb * 72 - (y * 8 + c * 4 + zm) * TXT
    valid = col < TXT
    loss_row = jnp.zeros((1, LANES), F32)
    inner = jnp.zeros((1, LANES), F32)

    def from_core(k, yy):
        arrived(ic_recv.at[yy], ic_rs.at[yy])
        total = iown[yy] + ic_recv[yy].astype(F32)
        if k < 3:
            iy_send[yy] = total.astype(BF16)
            send(iy_send.at[yy], iy_recv.at[y], (iy_ss, k), iy_rs.at[y], dev(y=yy))
        return total

    before = None
    for k, d in enumerate((2, 1, 3, 0)):
        yy = turn(y, d)
        arrived(xz.at[yy, cp], xc_rs.at[yy])
        for side_of in range(2):
            for q in range(4):
                first = side_of * HALF + q * ROWS
                xf[first : first + ROWS, :] = xz[yy, side_of, q].astype(F32)
        xs[yy] = xf[...].astype(BF16)
        slab = xs[yy]
        raw = dot(slab, tt[...], ((1,), (0,)))
        logits = raw * (sharpness * inv_txt) + offset
        diagonal = ahead == -144 * yy
        sign = jnp.where(diagonal, -1.0, 1.0)
        u = sign * logits
        e = jnp.exp(-jnp.abs(u))
        soft = jnp.maximum(u, 0.0) + jnp.log1p(e)
        loss_row += jnp.sum(jnp.where(valid, soft, 0.0), axis=0, keepdims=True)
        w = sign * (jnp.where(u >= 0, 1.0, e) / (1.0 + e)) * sharpness
        w = jnp.where(valid, w, 0.0)
        wb = w.astype(BF16)
        inner += jnp.sum(wb.astype(F32) * raw, axis=0, keepdims=True)
        w1[yy] = wb
        term[...] = dot((w * inv_txt).astype(BF16), tt[...], ((1,), (1,)))
        ic_send[yy] = term[pl.ds(pl.multiple_of(cp * HALF, 8), HALF), :].astype(BF16)
        send(ic_send.at[yy], ic_recv.at[yy], (ic_ss, k), ic_rs.at[yy], dev(c=cp))
        iown[yy] = term[pl.ds(pl.multiple_of(c * HALF, 8), HALF), :]
        if before is not None:
            from_core(*before)
        before = (k, yy)

    def loss_send(stage, place, others, value):
        ls[stage, place] = jnp.full((8, 128), value, F32)
        for k, peer in enumerate(others):
            send(ls.at[stage, place], ls.at[stage, place], (ls_ss, stage, k), ls_rs.at[stage, place], peer)

    def loss_wait(stage, places, n):
        for q in places:
            arrived(ls.at[stage, q], ls_rs.at[stage, q])
        total = ls[stage, 0]
        for q in range(1, n):
            total += ls[stage, q]
        return total

    loss_send(0, c, [dev(c=cp)], jnp.sum(loss_row))

    weights = w1[...].reshape(4 * SLAB, LANES)
    for q in range(3):
        part = xs[:, :, q * 384 : (q + 1) * 384].reshape(4 * SLAB, 384)
        dtf[q * 384 : (q + 1) * 384, :] = dot(part, weights, ((0,), (0,)))

    inner_tile = jnp.concatenate([inner[:, j * 128 : (j + 1) * 128] for j in range(3)] + [jnp.zeros((5, 128), F32)], axis=0)

    def features(xx, h, cc):
        rows = pl.ds(pl.multiple_of((xx * 4 + h * 2 + cc) * COLS, 8), COLS)
        return densify([dtf[rows, j * 128 : (j + 1) * 128] for j in range(3)])

    for j, h in enumerate((zhp, zh)):
        for d in (2, 1, 3):
            xx = turn(x, d)
            for cc in range(2):
                tx_send[xx, h, cc] = pack(features(xx, h, cc), inner_tile)
            send(tx_send.at[xx, h], tx_recv.at[x, h], (tx_ss, j, d - 1), tx_rs.at[x, h], dev(x=xx))

    total = from_core(*before)
    loss_v = loss_wait(0, [cp], 2)
    loss_send(1, zh * 2 + zb, [dev(zh=zhp), dev(zb=zbp), dev(zh=zhp, zb=zbp)], loss_v)
    for d in order:
        q = turn(y, d)
        arrived(iy_recv.at[q], iy_rs.at[q])
        total += iy_recv[q].astype(F32)
    xf[0:HALF, :] = total
    for q in range(4):
        iz_send[q] = xf[q * ROWS : (q + 1) * ROWS, :].astype(BF16)
    for k, d in enumerate((2, 1, 3)):
        q = turn(zm, d)
        send(iz_send.at[q], iz_recv.at[zm], (iz_ss, k), iz_rs.at[zm], dev(zm=q))
    loss_v = loss_wait(1, [zhp * 2 + zb, zh * 2 + zbp, zhp * 2 + zbp], 4)
    loss_send(2, y, [dev(y=turn(y, d)) for d in order], loss_v)

    for j, h in enumerate((zhp, zh)):
        sums = [features(x, h, cc) for cc in range(2)]
        inn = inner_tile
        for d in order:
            xx = turn(x, d)
            arrived(tx_recv.at[xx, h], tx_rs.at[xx, h])
            for cc in range(2):
                more, more_inn = unpack(tx_recv[xx, h, cc])
                sums[cc] += more
            inn += more_inn
        for cc in range(2):
            tf_send[j, cc] = pack(sums[cc], inn)

        @pl.when(is_guest)
        def _():
            for cc in range(2):
                send(tf_send.at[j, cc], tf_recv.at[zh, zb], (tf_ss, j, cc), tf_rs.at[zh, zb], dev(zh=h, zb=zbp, c=cc),
                     "guest", lambda: tf_send.at[0, 0])

        @pl.when(is_home)
        def _():
            if j == 0:
                for cc in range(2):
                    send(tf_send.at[j, cc], tf_recv.at[zh, zb], (tf_ss, j, cc), tf_rs.at[zh, zb], dev(zh=h, c=cc),
                         "home", lambda: tf_send.at[0, 0])
            else:
                send(tf_send.at[j, cp], tf_recv.at[zh, zb], (tf_ss, j, 0), tf_rs.at[zh, zb], dev(c=cp),
                     "home", lambda: tf_send.at[0, 0])
                for cc in range(2):
                    @pl.when(c == cc)
                    def _():
                        fin[0:DENSE] = sums[cc]
                        fin[DENSE:PIECE] = inn

        if j == 0:
            loss_v = loss_wait(2, [turn(y, d) for d in order], 4)
            loss_send(3, zm, [dev(zm=turn(zm, d)) for d in order], loss_v)

    total = iz_send[zm].astype(F32)
    for d in order:
        q = turn(zm, d)
        arrived(iz_recv.at[q], iz_rs.at[q])
        total += iz_recv[q].astype(F32)
    own_image = images[...].astype(F32)
    img_norm = lax.rsqrt(jnp.sum(own_image * own_image, axis=1, keepdims=True) + EPS)
    img_inner = jnp.sum(own_image * total, axis=1, keepdims=True)
    img_out[...] = img_norm * total - own_image * (img_norm * img_norm * img_norm * img_inner)
    loss_v = loss_wait(3, [turn(zm, d) for d in order], 4)
    loss_send(4, x, [dev(x=turn(x, d)) for d in order], loss_v)

    @pl.when(is_guest)
    def _():
        arrived(inv_far, inv_rs)
        inv_own[...] = inv_far[...]
        arrived(tf_recv.at[zh, zb], tf_rs.at[zh, zb])
        data, inn = unpack(tf_recv[zh, zb])
        fin[0:DENSE] = data
        fin[DENSE:PIECE] = inn

    data = fin[0:DENSE]
    inn = fin[DENSE:PIECE]
    for h, b in ((zh, zbp), (zhp, zbp), (zhp, zb)):
        arrived(tf_recv.at[h, b], tf_rs.at[h, b])
        more, more_inn = unpack(tf_recv[h, b])
        data += more
        inn += more_inn
    columns = (data[0:72], data[72:144], last_tile(data[144:DENSE]))
    for j in range(3):
        norm = inv_own[0:1, j * 128 : (j + 1) * 128]
        tpad[:, j * 128 : (j + 1) * 128] = norm * columns[j] - tpad[:, j * 128 : (j + 1) * 128] * (
            norm * norm * norm * inn[j : j + 1]
        )
    txt_out[...] = tpad[:, 0:TXT]
    loss_v = loss_wait(4, [turn(x, d) for d in order], 4)
    loss_out[0] = jnp.max(loss_v) / PAIRS

    sent("all")

    @pl.when(is_home)
    def _():
        sent("home")

    @pl.when(is_guest)
    def _():
        sent("guest")


def per_device(images, texts, logit_scale, bias):
    vmem = pl.BlockSpec(memory_space=pltpu.VMEM)
    smem = pl.BlockSpec(memory_space=pltpu.SMEM)
    sem = pltpu.SemaphoreType.DMA
    loss, grad_images, grad_texts = pl.pallas_call(
        kernel,
        out_shape=(
            jax.ShapeDtypeStruct((1,), F32),
            jax.ShapeDtypeStruct((ROWS, D), F32),
            jax.ShapeDtypeStruct((COLS, TXT), F32),
        ),
        in_specs=[vmem, vmem, smem, smem],
        out_specs=(smem, vmem, vmem),
        scratch_shapes=[
            pltpu.VMEM((4, 2, 4, ROWS, D), BF16),
            pltpu.VMEM((SLAB, D), F32),
            pltpu.VMEM((4, SLAB, D), BF16),
            pltpu.VMEM((DENSE, 128), BF16),
            pltpu.VMEM((COLS, LANES), F32),
            pltpu.VMEM((4, 2, 2, DENSE, 128), BF16),
            pltpu.VMEM((D, LANES), BF16),
            pltpu.VMEM((8, LANES), F32),
            pltpu.VMEM((8, LANES), F32),
            pltpu.VMEM((4, SLAB, LANES), BF16),
            pltpu.VMEM((SLAB, D), F32),
            pltpu.VMEM((4, HALF, D), F32),
            pltpu.VMEM((4, HALF, D), BF16),
            pltpu.VMEM((4, HALF, D), BF16),
            pltpu.VMEM((4, HALF, D), BF16),
            pltpu.VMEM((4, HALF, D), BF16),
            pltpu.VMEM((4, ROWS, D), BF16),
            pltpu.VMEM((4, ROWS, D), BF16),
            pltpu.VMEM((D, LANES), F32),
            pltpu.VMEM((4, 2, 2, PIECE, 128), BF16),
            pltpu.VMEM((4, 2, 2, PIECE, 128), BF16),
            pltpu.VMEM((2, 2, PIECE, 128), BF16),
            pltpu.VMEM((2, 2, PIECE, 128), BF16),
            pltpu.VMEM((PIECE, 128), F32),
            pltpu.VMEM((5, 4, 8, 128), F32),
            sem((15,)), sem((4, 4)),
            sem((4,)), sem((4,)),
            sem((17,)), sem((4, 2, 2)),
            sem, sem,
            sem((4,)), sem((4,)),
            sem((3,)), sem((4,)),
            sem((3,)), sem((4,)),
            sem((2, 3)), sem((4, 2)),
            sem((2, 2)), sem((2, 2)),
            sem((5, 3)), sem((5, 4)),
        ],
        compiler_params=pltpu.CompilerParams(
            collective_id=0, has_side_effects=True, vmem_limit_bytes=48 * 1024 * 1024
        ),
        name="siglip",
    )(images, texts.T, logit_scale, bias)
    return loss, grad_images, grad_texts.T


def solution(mesh):
    return jax.shard_map(
        per_device,
        mesh=mesh,
        in_specs=(P(("img", "txt"), None), P("txt", "img"), P(), P()),
        out_specs=(P(), P(("img", "txt"), None), P("txt", "img")),
        check_vma=False,
    )
```

time: 85.5 us -> 75.1 us (0.88)
  the two profiles are of different devices: /device:TPU:32 before, /device:TPU:1 now
where the time goes in v3:
time: 75.1 us; the launch traced here: 74.9 us
  Pallas kernels  68.3 us (91%)
  between operations  3.7 us (5%)
  local copies, waits for them, and re-layouts  2.91 us (4%)
    pallas_call x1, Pallas kernels, per_device(): pl.pallas_call(kernel, out_shape=(jax.ShapeDtypeStruct((1,), F32), jax.Sh...  68.3 us
    unnamed x6, local copies, waits for them, and re-layouts  2.91 us

profile of v3, /device:TPU:1, one launch (start us, length us, event | category | flops | bytes accessed | tf_op | source)
XLA Modules:
  0.0 74.9 jit_solution(6297591928808606902)
XLA Ops:
  1.9 0.0 copy-start
  1.9 0.8 %copy-done = bf16[18,1152]{1,0:T(8,128)(2,1)S(1)} copy-done((bf16[18,1152]{1,0:T(8,128)(2,1)S(1)}, bf16[18,1152]{1,0:T(8,128)(2,1)}, u32[]{:S(2)}) %copy-start) | copy-done | bytes 41496
  2.7 0.0 copy-start.1
  2.7 0.8 %copy-done.1 = bf16[288,72]{0,1:T(8,128)(2,1)S(1)} copy-done((bf16[288,72]{0,1:T(8,128)(2,1)S(1)}, bf16[288,72]{0,1:T(8,128)(2,1)}, u32[]{:S(2)}) %copy-start.1) | copy-done | bytes 41496
  3.6 68.3 %siglip.1 = (f32[1]{0:T(128)}, f32[18,1152]{1,0:T(8,128)S(1)}, f32[72,288]{1,0:T(8,128)S(1)}) custom-call(bf16[18,1152]{1,0:T(8,128)(2,1)S(1)} %copy-done, bf16[72,288]{1,0:T(8,128)(2,1)S(1)} %bitcast.3, f32[1]{0:T(128)S(6)} %copy.10.scale, f32[1]{0:T(128)S(6)} %copy.11.bias), custom_call_target="tpu_custom_call" | custom-call | tf_op jit(solution)/shard_map/siglip/pallas_call | solution.py:409
  72.5 0.6 copy.13
  73.1 0.6 copy.14
Async XLA Ops:
  1.9 0.8 %copy-start = (bf16[18,1152]{1,0:T(8,128)(2,1)S(1)}, bf16[18,1152]{1,0:T(8,128)(2,1)}, u32[]{:S(2)}) copy-start(bf16[18,1152]{1,0:T(8,128)(2,1)} %images.1) | copy-start | bytes 124420
  2.7 0.8 %copy-start.1 = (bf16[288,72]{0,1:T(8,128)(2,1)S(1)}, bf16[288,72]{0,1:T(8,128)(2,1)}, u32[]{:S(2)}) copy-start(bf16[288,72]{0,1:T(8,128)(2,1)} %param.5) | copy-start | bytes 124420

commit v4 on v3

--- a/solution.py
+++ b/solution.py
@@ -53,10 +53,10 @@
 
 def kernel(
     images, texts, scale, bias, loss_out, img_out, txt_out,
-    xz, xf, xs, tp, tpad, ts, tt, inv_own, inv_far, w1, term, iown, ic_send, ic_recv, iy_send, iy_recv, iz_send, iz_recv,
-    dtf, tx_send, tx_recv, tf_send, tf_recv, fin, ls,
+    xz, xf, xs, tp, tpad, ts, tt, inv_own, inv_far, w1, w2, term, iown, ic_send, ic_recv, iy_send, iy_recv, iz_send, iz_recv,
+    dtf, tx_send, tx_recv, tf_send, tf_recv, tg_recv, tsum, fin, ls,
     xz_ss, xz_rs, xc_ss, xc_rs, ts_ss, ts_rs, inv_ss, inv_rs, ic_ss, ic_rs, iy_ss, iy_rs, iz_ss, iz_rs,
-    tx_ss, tx_rs, tf_ss, tf_rs, ls_ss, ls_rs,
+    tx_ss, tx_rs, tf_ss, tf_rs, tg_rs, ls_ss, ls_rs,
 ):
     i = lax.axis_index("img")
     t = lax.axis_index("txt")
@@ -160,9 +160,13 @@
         t_send("guest", x, zh, c, dev(zh=zhp, zb=zbp, c=cp), True)
         t_send("guest", x, zh, c, dev(c=cp), True)
 
+    x_over_y(zm)
+    for who in ("home", "guest"):
+        pending[who] = pending[who][2:]
+    for k in range(2):
+        copy(tp, tp, ts_ss.at[k], ls_rs.at[0, 0], dev(c=cp)).wait_send()
     for d in (1, 3, 2):
         x_send(zm, dev(zm=turn(zm, d)))
-    x_over_y(zm)
 
     @pl.when(is_home)
     def _():
@@ -198,20 +202,28 @@
         for q in range(4):
             x_wait(yy, turn(zm, q))
         x_to_core(d, yy)
+    for d in (0, 1, 3, 2):
+        yy = turn(y, d)
+        arrived(xz.at[yy, cp], xc_rs.at[yy])
+        for side_of in range(2):
+            for q in range(4):
+                first = side_of * HALF + q * ROWS
+                xf[first : first + ROWS, :] = xz[yy, side_of, q].astype(F32)
+        xs[yy] = xf[...].astype(BF16)
+
+    square = jnp.zeros((8, LANES), F32)
     for h in (zh, zhp):
-        for cc in range(2):
-            for d in order:
-                t_wait(turn(x, d), h, cc)
-
-    square = jnp.zeros((8, LANES), F32)
-    for j in range(8):
-        halves = []
-        for cc in range(2):
-            block = ts[j // 2, j % 2, cc].astype(F32)
-            halves.append(jnp.concatenate([block[0:72], block[72:144], last_tile(block[144:DENSE])], axis=1))
-        both = jnp.concatenate(halves, axis=0)
-        tt[j * 144 : (j + 1) * 144, :] = both.astype(BF16)
-        square += jnp.sum((both * both).reshape(18, 8, LANES), axis=0)
+        for d in (0, 1, 3, 2):
+            xx = turn(x, d)
+            halves = []
+            for cc in range(2):
+                if d:
+                    t_wait(xx, h, cc)
+                block = ts[xx, h, cc].astype(F32)
+                halves.append(jnp.concatenate([block[0:72], block[72:144], last_tile(block[144:DENSE])], axis=1))
+            both = jnp.concatenate(halves, axis=0)
+            tt[pl.ds(pl.multiple_of((xx * 2 + h) * 144, 16), 144), :] = both.astype(BF16)
+            square += jnp.sum((both * both).reshape(18, 8, LANES), axis=0)
     inv_txt = lax.rsqrt(jnp.sum(square, axis=0, keepdims=True) + EPS)
     inv_own[...] = jnp.broadcast_to(inv_txt, (8, LANES))
 
@@ -227,23 +239,8 @@
     loss_row = jnp.zeros((1, LANES), F32)
     inner = jnp.zeros((1, LANES), F32)
 
-    def from_core(k, yy):
-        arrived(ic_recv.at[yy], ic_rs.at[yy])
-        total = iown[yy] + ic_recv[yy].astype(F32)
-        if k < 3:
-            iy_send[yy] = total.astype(BF16)
-            send(iy_send.at[yy], iy_recv.at[y], (iy_ss, k), iy_rs.at[y], dev(y=yy))
-        return total
-
-    before = None
-    for k, d in enumerate((2, 1, 3, 0)):
+    for d in (0, 1, 3, 2):
         yy = turn(y, d)
-        arrived(xz.at[yy, cp], xc_rs.at[yy])
-        for side_of in range(2):
-            for q in range(4):
-                first = side_of * HALF + q * ROWS
-                xf[first : first + ROWS, :] = xz[yy, side_of, q].astype(F32)
-        xs[yy] = xf[...].astype(BF16)
         slab = xs[yy]
         raw = dot(slab, tt[...], ((1,), (0,)))
         logits = raw * (sharpness * inv_txt) + offset
@@ -258,13 +255,7 @@
         wb = w.astype(BF16)
         inner += jnp.sum(wb.astype(F32) * raw, axis=0, keepdims=True)
         w1[yy] = wb
-        term[...] = dot((w * inv_txt).astype(BF16), tt[...], ((1,), (1,)))
-        ic_send[yy] = term[pl.ds(pl.multiple_of(cp * HALF, 8), HALF), :].astype(BF16)
-        send(ic_send.at[yy], ic_recv.at[yy], (ic_ss, k), ic_rs.at[yy], dev(c=cp))
-        iown[yy] = term[pl.ds(pl.multiple_of(c * HALF, 8), HALF), :]
-        if before is not None:
-            from_core(*before)
-        before = (k, yy)
+        w2[yy] = (w * inv_txt).astype(BF16)
 
     def loss_send(stage, place, others, value):
         ls[stage, place] = jnp.full((8, 128), value, F32)
@@ -292,16 +283,87 @@
         rows = pl.ds(pl.multiple_of((xx * 4 + h * 2 + cc) * COLS, 8), COLS)
         return densify([dtf[rows, j * 128 : (j + 1) * 128] for j in range(3)])
 
-    for j, h in enumerate((zhp, zh)):
+    def which(j, m):
+        h = jnp.where(is_home, (zhp, zh)[j], m)
+        cc = jnp.where(is_home, m, (1 - zh, zh)[j])
+        return h, cc
+
+    for j in range(2):
         for d in (2, 1, 3):
             xx = turn(x, d)
-            for cc in range(2):
-                tx_send[xx, h, cc] = pack(features(xx, h, cc), inner_tile)
-            send(tx_send.at[xx, h], tx_recv.at[x, h], (tx_ss, j, d - 1), tx_rs.at[x, h], dev(x=xx))
+            for m in range(2):
+                tx_send[xx, j, m] = pack(features(xx, *which(j, m)), inner_tile)
+            send(tx_send.at[xx, j], tx_recv.at[x, j], (tx_ss, j, d - 1), tx_rs.at[x, j], dev(x=xx))
+
+    def from_core(k, yy):
+        arrived(ic_recv.at[yy], ic_rs.at[yy])
+        total = iown[yy] + ic_recv[yy].astype(F32)
+        if k < 3:
+            iy_send[yy] = total.astype(BF16)
+            send(iy_send.at[yy], iy_recv.at[y], (iy_ss, k), iy_rs.at[y], dev(y=yy))
+        return total
+
+    before = None
+    for k, d in enumerate((2, 1, 3, 0)):
+        yy = turn(y, d)
+        term[...] = dot(w2[yy], tt[...], ((1,), (1,)))
+        ic_send[yy] = term[pl.ds(pl.multiple_of(cp * HALF, 8), HALF), :].astype(BF16)
+        send(ic_send.at[yy], ic_recv.at[yy], (ic_ss, k), ic_rs.at[yy], dev(c=cp))
+        iown[yy] = term[pl.ds(pl.multiple_of(c * HALF, 8), HALF), :]
+        if before is not None:
+            from_core(*before)
+        before = (k, yy)
 
     total = from_core(*before)
     loss_v = loss_wait(0, [cp], 2)
     loss_send(1, zh * 2 + zb, [dev(zh=zhp), dev(zb=zbp), dev(zh=zhp, zb=zbp)], loss_v)
+    def to_owners(j):
+        sums = [features(x, *which(j, m)) for m in range(2)]
+        inn = inner_tile
+        for d in order:
+            xx = turn(x, d)
+            arrived(tx_recv.at[xx, j], tx_rs.at[xx, j])
+            for m in range(2):
+                more, more_inn = unpack(tx_recv[xx, j, m])
+                sums[m] += more
+            inn += more_inn
+        if j == 0:
+            for m in range(2):
+                tf_send[0, m] = pack(sums[m], inn)
+
+            @pl.when(is_home)
+            def _():
+                for m in range(2):
+                    send(tf_send.at[0, m], tg_recv.at[zh], (tf_ss, 0, m), tg_rs.at[zh], dev(zh=m, zb=zbp),
+                         "home", lambda: tf_send.at[0, 0])
+
+            @pl.when(is_guest)
+            def _():
+                for m in range(2):
+                    send(tf_send.at[0, m], tf_recv.at[zh], (tf_ss, 0, m), tf_rs.at[zh, 0], dev(zh=m, zb=zbp, c=1 - zh),
+                         "guest", lambda: tf_send.at[0, 0])
+        else:
+            for m in range(2):
+                tsum[m, 0:DENSE] = sums[m]
+                tsum[m, DENSE:PIECE] = inn
+
+            @pl.when(is_home)
+            def _():
+                tf_send[1, 0] = pack(tsum[cp, 0:DENSE], tsum[cp, DENSE:PIECE])
+                send(tf_send.at[1, 0], tf_recv.at[2], (tf_ss, 1, 0), tf_rs.at[0, 1], dev(c=cp),
+                     "home", lambda: tf_send.at[0, 0])
+                fin[...] = tsum[c]
+
+            @pl.when(is_guest)
+            def _():
+                for m in range(2):
+                    arrived(tg_recv.at[1 - m], tg_rs.at[1 - m])
+                    more, more_inn = unpack(tg_recv[1 - m])
+                    tf_send[1, m] = pack(tsum[m, 0:DENSE] + more, tsum[m, DENSE:PIECE] + more_inn)
+                    send(tf_send.at[1, m], tf_recv.at[zh], (tf_ss, 1, m), tf_rs.at[zh, 0], dev(zh=m, zb=zbp, c=zh),
+                         "guest", lambda: tf_send.at[0, 0])
+
+    to_owners(0)
     for d in order:
         q = turn(y, d)
         arrived(iy_recv.at[q], iy_rs.at[q])
@@ -315,43 +377,9 @@
     loss_v = loss_wait(1, [zhp * 2 + zb, zh * 2 + zbp, zhp * 2 + zbp], 4)
     loss_send(2, y, [dev(y=turn(y, d)) for d in order], loss_v)
 
-    for j, h in enumerate((zhp, zh)):
-        sums = [features(x, h, cc) for cc in range(2)]
-        inn = inner_tile
-        for d in order:
-            xx = turn(x, d)
-            arrived(tx_recv.at[xx, h], tx_rs.at[xx, h])
-            for cc in range(2):
-                more, more_inn = unpack(tx_recv[xx, h, cc])
-                sums[cc] += more
-            inn += more_inn
-        for cc in range(2):
-            tf_send[j, cc] = pack(sums[cc], inn)
-
-        @pl.when(is_guest)
-        def _():
-            for cc in range(2):
-                send(tf_send.at[j, cc], tf_recv.at[zh, zb], (tf_ss, j, cc), tf_rs.at[zh, zb], dev(zh=h, zb=zbp, c=cc),
-                     "guest", lambda: tf_send.at[0, 0])
-
-        @pl.when(is_home)
-        def _():
-            if j == 0:
-                for cc in range(2):
-                    send(tf_send.at[j, cc], tf_recv.at[zh, zb], (tf_ss, j, cc), tf_rs.at[zh, zb], dev(zh=h, c=cc),
-                         "home", lambda: tf_send.at[0, 0])
-            else:
-                send(tf_send.at[j, cp], tf_recv.at[zh, zb], (tf_ss, j, 0), tf_rs.at[zh, zb], dev(c=cp),
-                     "home", lambda: tf_send.at[0, 0])
-                for cc in range(2):
-                    @pl.when(c == cc)
-                    def _():
-                        fin[0:DENSE] = sums[cc]
-                        fin[DENSE:PIECE] = inn
-
-        if j == 0:
-            loss_v = loss_wait(2, [turn(y, d) for d in order], 4)
-            loss_send(3, zm, [dev(zm=turn(zm, d)) for d in order], loss_v)
+    to_owners(1)
+    loss_v = loss_wait(2, [turn(y, d) for d in order], 4)
+    loss_send(3, zm, [dev(zm=turn(zm, d)) for d in order], loss_v)
 
     total = iz_send[zm].astype(F32)
     for d in order:
@@ -369,16 +397,16 @@
     def _():
         arrived(inv_far, inv_rs)
         inv_own[...] = inv_far[...]
-        arrived(tf_recv.at[zh, zb], tf_rs.at[zh, zb])
-        data, inn = unpack(tf_recv[zh, zb])
+        arrived(tf_recv.at[2], tf_rs.at[0, 1])
+        data, inn = unpack(tf_recv[2])
         fin[0:DENSE] = data
         fin[DENSE:PIECE] = inn
 
     data = fin[0:DENSE]
     inn = fin[DENSE:PIECE]
-    for h, b in ((zh, zbp), (zhp, zbp), (zhp, zb)):
-        arrived(tf_recv.at[h, b], tf_rs.at[h, b])
-        more, more_inn = unpack(tf_recv[h, b])
+    for g in (1 - c, c):
+        arrived(tf_recv.at[g], tf_rs.at[g, 0])
+        more, more_inn = unpack(tf_recv[g])
         data += more
         inn += more_inn
     columns = (data[0:72], data[72:144], last_tile(data[144:DENSE]))
@@ -389,7 +417,7 @@
         )
     txt_out[...] = tpad[:, 0:TXT]
     loss_v = loss_wait(4, [turn(x, d) for d in order], 4)
-    loss_out[0] = jnp.max(loss_v) / PAIRS
+    loss_out[...] = loss_v / PAIRS
 
     sent("all")
 
@@ -409,12 +437,12 @@
     loss, grad_images, grad_texts = pl.pallas_call(
         kernel,
         out_shape=(
-            jax.ShapeDtypeStruct((1,), F32),
+            jax.ShapeDtypeStruct((8, 128), F32),
             jax.ShapeDtypeStruct((ROWS, D), F32),
             jax.ShapeDtypeStruct((COLS, TXT), F32),
         ),
         in_specs=[vmem, vmem, smem, smem],
-        out_specs=(smem, vmem, vmem),
+        out_specs=(vmem, vmem, vmem),
         scratch_shapes=[
             pltpu.VMEM((4, 2, 4, ROWS, D), BF16),
             pltpu.VMEM((SLAB, D), F32),
@@ -425,6 +453,7 @@
             pltpu.VMEM((D, LANES), BF16),
             pltpu.VMEM((8, LANES), F32),
             pltpu.VMEM((8, LANES), F32),
+            pltpu.VMEM((4, SLAB, LANES), BF16),
             pltpu.VMEM((4, SLAB, LANES), BF16),
             pltpu.VMEM((SLAB, D), F32),
             pltpu.VMEM((4, HALF, D), F32),
@@ -438,7 +467,9 @@
             pltpu.VMEM((4, 2, 2, PIECE, 128), BF16),
             pltpu.VMEM((4, 2, 2, PIECE, 128), BF16),
             pltpu.VMEM((2, 2, PIECE, 128), BF16),
-            pltpu.VMEM((2, 2, PIECE, 128), BF16),
+            pltpu.VMEM((3, PIECE, 128), BF16),
+            pltpu.VMEM((2, PIECE, 128), BF16),
+            pltpu.VMEM((2, PIECE, 128), F32),
             pltpu.VMEM((PIECE, 128), F32),
             pltpu.VMEM((5, 4, 8, 128), F32),
             sem((15,)), sem((4, 4)),
@@ -449,7 +480,7 @@
             sem((3,)), sem((4,)),
             sem((3,)), sem((4,)),
             sem((2, 3)), sem((4, 2)),
-            sem((2, 2)), sem((2, 2)),
+            sem((2, 2)), sem((2, 2)), sem((2,)),
             sem((5, 3)), sem((5, 4)),
         ],
         compiler_params=pltpu.CompilerParams(
@@ -457,7 +488,7 @@
         ),
         name="siglip",
     )(images, texts.T, logit_scale, bias)
-    return loss, grad_images, grad_texts.T
+    return loss[0, 0:1], grad_images, grad_texts.T
 
 
 def solution(mesh):

time: 75.1 us -> 70.1 us (0.933)
  Pallas kernels: 68.3 us -> 64.5 us
  between operations: 3.7 us -> 1.94 us
    pallas_call x1, Pallas kernels: 68.3 us -> 64.5 us  [per_device(): pl.pallas_call(kernel, out_shape=(jax.ShapeDtypeStruct((8, 128), F32), ja...]
where the time goes in v4:
time: 70.1 us; the launch traced here: 69.9 us
  Pallas kernels  64.5 us (92%)
  local copies, waits for them, and re-layouts  3.42 us (5%)
  between operations  1.94 us (3%)
    pallas_call x1, Pallas kernels, per_device(): pl.pallas_call(kernel, out_shape=(jax.ShapeDtypeStruct((8, 128), F32), ja...  64.5 us
    unnamed x6, local copies, waits for them, and re-layouts  2.91 us

profile of v4, /device:TPU:1, one launch (start us, length us, event | category | flops | bytes accessed | tf_op | source)
XLA Modules:
  0.0 69.9 jit_solution(15416615724895690137)
XLA Ops:
  1.9 0.0 copy-start
  1.9 0.8 %copy-done = bf16[18,1152]{1,0:T(8,128)(2,1)S(1)} copy-done((bf16[18,1152]{1,0:T(8,128)(2,1)S(1)}, bf16[18,1152]{1,0:T(8,128)(2,1)}, u32[]{:S(2)}) %copy-start) | copy-done | bytes 41496
  2.7 0.0 copy-start.1
  2.7 0.8 %copy-done.1 = bf16[288,72]{0,1:T(8,128)(2,1)S(1)} copy-done((bf16[288,72]{0,1:T(8,128)(2,1)S(1)}, bf16[288,72]{0,1:T(8,128)(2,1)}, u32[]{:S(2)}) %copy-start.1) | copy-done | bytes 41496
  3.6 64.5 %siglip.1 = (f32[8,128]{1,0:T(8,128)S(1)}, f32[18,1152]{1,0:T(8,128)S(1)}, f32[72,288]{1,0:T(8,128)S(1)}) custom-call(bf16[18,1152]{1,0:T(8,128)(2,1)S(1)} %copy-done, bf16[72,288]{1,0:T(8,128)(2,1)S(1)} %bitcast.4, f32[1]{0:T(128)S(6)} %copy.9.scale, f32[1]{0:T(128)S(6)} %copy.10.bias), custom_call_target="tpu_custom_call" | custom-call | tf_op jit(solution)/shard_map/siglip/pallas_call | solution.py:437
  68.1 0.5 slice.3
  68.6 0.6 copy.11
  69.3 0.6 copy.12
Async XLA Ops:
  1.9 0.8 %copy-start = (bf16[18,1152]{1,0:T(8,128)(2,1)S(1)}, bf16[18,1152]{1,0:T(8,128)(2,1)}, u32[]{:S(2)}) copy-start(bf16[18,1152]{1,0:T(8,128)(2,1)} %images.1) | copy-start | bytes 124420
  2.7 0.8 %copy-start.1 = (bf16[288,72]{0,1:T(8,128)(2,1)S(1)}, bf16[288,72]{0,1:T(8,128)(2,1)}, u32[]{:S(2)}) copy-start(bf16[288,72]{0,1:T(8,128)(2,1)} %param.5) | copy-start | bytes 124420

commit v5 on v4

--- a/solution.py
+++ b/solution.py
@@ -12,6 +12,7 @@
 D = 1152
 PAIRS = 9216
 ROWS = 18
+XPIECE = 168
 HALF = 72
 SLAB = 144
 COLS = 72
@@ -53,7 +54,7 @@
 
 def kernel(
     images, texts, scale, bias, loss_out, img_out, txt_out,
-    xz, xf, xs, tp, tpad, ts, tt, inv_own, inv_far, w1, w2, term, iown, ic_send, ic_recv, iy_send, iy_recv, iz_send, iz_recv,
+    xz, xg, xf, xs, tp, tpad, ts, tt, inv_own, inv_far, w1, w2, term, iown, ic_send, ic_recv, iy_send, iy_recv, iz_send, iz_recv,
     dtf, tx_send, tx_recv, tf_send, tf_recv, tg_recv, tsum, fin, ls,
     xz_ss, xz_rs, xc_ss, xc_rs, ts_ss, ts_rs, inv_ss, inv_rs, ic_ss, ic_rs, iy_ss, iy_rs, iz_ss, iz_rs,
     tx_ss, tx_rs, tf_ss, tf_rs, tg_rs, ls_ss, ls_rs,
@@ -104,9 +105,20 @@
     sharpness = scale[0]
     offset = bias[0]
 
+    def to_dense(block, first):
+        for j in range(9):
+            block[j * ROWS : (j + 1) * ROWS, :] = xf[first : first + ROWS, j * 128 : (j + 1) * 128]
+
+    def from_dense(block, first):
+        for j in range(9):
+            xf[first : first + ROWS, j * 128 : (j + 1) * 128] = block[j * ROWS : (j + 1) * ROWS, :]
+
+    xg[...] = jnp.zeros((8, XPIECE, 128), F32)
     own_image = images[...].astype(F32)
     img_norm = lax.rsqrt(jnp.sum(own_image * own_image, axis=1, keepdims=True) + EPS)
-    xz[y, c, zm] = (own_image * img_norm).astype(BF16)
+    xf[0:ROWS, :] = own_image * img_norm
+    to_dense(xg.at[0], 0)
+    xz[y, c, zm] = xg[0].astype(BF16)
     tpad[...] = jnp.zeros((COLS, LANES), F32)
     tpad[:, 0:TXT] = texts[...].astype(F32)
     tp[...] = densify([tpad[:, j * 128 : (j + 1) * 128] for j in range(3)]).astype(BF16)
@@ -205,10 +217,9 @@
     for d in (0, 1, 3, 2):
         yy = turn(y, d)
         arrived(xz.at[yy, cp], xc_rs.at[yy])
-        for side_of in range(2):
-            for q in range(4):
-                first = side_of * HALF + q * ROWS
-                xf[first : first + ROWS, :] = xz[yy, side_of, q].astype(F32)
+        xg[...] = xz[yy].reshape(8, XPIECE, 128).astype(F32)
+        for q in range(8):
+            from_dense(xg.at[q], q * ROWS)
         xs[yy] = xf[...].astype(BF16)
 
     square = jnp.zeros((8, LANES), F32)
@@ -370,7 +381,8 @@
         total += iy_recv[q].astype(F32)
     xf[0:HALF, :] = total
     for q in range(4):
-        iz_send[q] = xf[q * ROWS : (q + 1) * ROWS, :].astype(BF16)
+        to_dense(xg.at[q], q * ROWS)
+        iz_send[q] = xg[q].astype(BF16)
     for k, d in enumerate((2, 1, 3)):
         q = turn(zm, d)
         send(iz_send.at[q], iz_recv.at[zm], (iz_ss, k), iz_rs.at[zm], dev(zm=q))
@@ -386,6 +398,9 @@
         q = turn(zm, d)
         arrived(iz_recv.at[q], iz_rs.at[q])
         total += iz_recv[q].astype(F32)
+    xg[0] = total
+    from_dense(xg.at[0], 0)
+    total = xf[0:ROWS, :]
     own_image = images[...].astype(F32)
     img_norm = lax.rsqrt(jnp.sum(own_image * own_image, axis=1, keepdims=True) + EPS)
     img_inner = jnp.sum(own_image * total, axis=1, keepdims=True)
@@ -444,7 +459,8 @@
         in_specs=[vmem, vmem, smem, smem],
         out_specs=(vmem, vmem, vmem),
         scratch_shapes=[
-            pltpu.VMEM((4, 2, 4, ROWS, D), BF16),
+            pltpu.VMEM((4, 2, 4, XPIECE, 128), BF16),
+            pltpu.VMEM((8, XPIECE, 128), F32),
             pltpu.VMEM((SLAB, D), F32),
             pltpu.VMEM((4, SLAB, D), BF16),
             pltpu.VMEM((DENSE, 128), BF16),
@@ -461,8 +477,8 @@
             pltpu.VMEM((4, HALF, D), BF16),
             pltpu.VMEM((4, HALF, D), BF16),
             pltpu.VMEM((4, HALF, D), BF16),
-            pltpu.VMEM((4, ROWS, D), BF16),
-            pltpu.VMEM((4, ROWS, D), BF16),
+            pltpu.VMEM((4, XPIECE, 128), BF16),
+            pltpu.VMEM((4, XPIECE, 128), BF16),
             pltpu.VMEM((D, LANES), F32),
             pltpu.VMEM((4, 2, 2, PIECE, 128), BF16),
             pltpu.VMEM((4, 2, 2, PIECE, 128), BF16),

time: 70.1 us -> 68.6 us (0.979)
  Pallas kernels: 64.5 us -> 63 us
    pallas_call x1, Pallas kernels: 64.5 us -> 63 us  [per_device(): pl.pallas_call(kernel, out_shape=(jax.ShapeDtypeStruct((8, 128), F32), ja...]
where the time goes in v5:
time: 68.6 us; the launch traced here: 68.4 us
  Pallas kernels  63 us (92%)
  local copies, waits for them, and re-layouts  3.42 us (5%)
  between operations  1.94 us (3%)
    pallas_call x1, Pallas kernels, per_device(): pl.pallas_call(kernel, out_shape=(jax.ShapeDtypeStruct((8, 128), F32), ja...  63 us
    unnamed x6, local copies, waits for them, and re-layouts  2.91 us

profile of v5, /device:TPU:1, one launch (start us, length us, event | category | flops | bytes accessed | tf_op | source)
XLA Modules:
  0.0 68.4 jit_solution(16068856155771593)
XLA Ops:
  1.9 0.0 copy-start
  1.9 0.8 %copy-done = bf16[18,1152]{1,0:T(8,128)(2,1)S(1)} copy-done((bf16[18,1152]{1,0:T(8,128)(2,1)S(1)}, bf16[18,1152]{1,0:T(8,128)(2,1)}, u32[]{:S(2)}) %copy-start) | copy-done | bytes 41496
  2.7 0.0 copy-start.1
  2.7 0.8 %copy-done.1 = bf16[288,72]{0,1:T(8,128)(2,1)S(1)} copy-done((bf16[288,72]{0,1:T(8,128)(2,1)S(1)}, bf16[288,72]{0,1:T(8,128)(2,1)}, u32[]{:S(2)}) %copy-start.1) | copy-done | bytes 41496
  3.6 63.0 %siglip.1 = (f32[8,128]{1,0:T(8,128)S(1)}, f32[18,1152]{1,0:T(8,128)S(1)}, f32[72,288]{1,0:T(8,128)S(1)}) custom-call(bf16[18,1152]{1,0:T(8,128)(2,1)S(1)} %copy-done, bf16[72,288]{1,0:T(8,128)(2,1)S(1)} %bitcast.4, f32[1]{0:T(128)S(6)} %copy.9.scale, f32[1]{0:T(128)S(6)} %copy.10.bias), custom_call_target="tpu_custom_call" | custom-call | tf_op jit(solution)/shard_map/siglip/pallas_call | solution.py:452
  66.6 0.5 slice.3
  67.1 0.6 copy.11
  67.8 0.6 copy.12
Async XLA Ops:
  1.9 0.8 %copy-start = (bf16[18,1152]{1,0:T(8,128)(2,1)S(1)}, bf16[18,1152]{1,0:T(8,128)(2,1)}, u32[]{:S(2)}) copy-start(bf16[18,1152]{1,0:T(8,128)(2,1)} %images.1) | copy-start | bytes 124420
  2.7 0.8 %copy-start.1 = (bf16[288,72]{0,1:T(8,128)(2,1)S(1)}, bf16[288,72]{0,1:T(8,128)(2,1)}, u32[]{:S(2)}) copy-start(bf16[288,72]{0,1:T(8,128)(2,1)} %param.5) | copy-start | bytes 124420

commit v6 on v5

--- a/solution.py
+++ b/solution.py
@@ -375,6 +375,8 @@
                          "guest", lambda: tf_send.at[0, 0])
 
     to_owners(0)
+    loss_v = loss_wait(1, [zhp * 2 + zb, zh * 2 + zbp, zhp * 2 + zbp], 4)
+    loss_send(2, y, [dev(y=turn(y, d)) for d in order], loss_v)
     for d in order:
         q = turn(y, d)
         arrived(iy_recv.at[q], iy_rs.at[q])
@@ -386,12 +388,12 @@
     for k, d in enumerate((2, 1, 3)):
         q = turn(zm, d)
         send(iz_send.at[q], iz_recv.at[zm], (iz_ss, k), iz_rs.at[zm], dev(zm=q))
-    loss_v = loss_wait(1, [zhp * 2 + zb, zh * 2 + zbp, zhp * 2 + zbp], 4)
-    loss_send(2, y, [dev(y=turn(y, d)) for d in order], loss_v)
-
-    to_owners(1)
     loss_v = loss_wait(2, [turn(y, d) for d in order], 4)
     loss_send(3, zm, [dev(zm=turn(zm, d)) for d in order], loss_v)
+
+    to_owners(1)
+    loss_v = loss_wait(3, [turn(zm, d) for d in order], 4)
+    loss_send(4, x, [dev(x=turn(x, d)) for d in order], loss_v)
 
     total = iz_send[zm].astype(F32)
     for d in order:
@@ -405,8 +407,6 @@
     img_norm = lax.rsqrt(jnp.sum(own_image * own_image, axis=1, keepdims=True) + EPS)
     img_inner = jnp.sum(own_image * total, axis=1, keepdims=True)
     img_out[...] = img_norm * total - own_image * (img_norm * img_norm * img_norm * img_inner)
-    loss_v = loss_wait(3, [turn(zm, d) for d in order], 4)
-    loss_send(4, x, [dev(x=turn(x, d)) for d in order], loss_v)
 
     @pl.when(is_guest)
     def _():

time: 68.6 us -> 67.7 us (0.987)
  Pallas kernels: 63 us -> 62.1 us
    pallas_call x1, Pallas kernels: 63 us -> 62.1 us  [per_device(): pl.pallas_call(kernel, out_shape=(jax.ShapeDtypeStruct((8, 128), F32), ja...]
where the time goes in v6:
time: 67.7 us; the launch traced here: 67.5 us
  Pallas kernels  62.1 us (92%)
  local copies, waits for them, and re-layouts  3.42 us (5%)
  between operations  1.94 us (3%)
    pallas_call x1, Pallas kernels, per_device(): pl.pallas_call(kernel, out_shape=(jax.ShapeDtypeStruct((8, 128), F32), ja...  62.1 us
    unnamed x6, local copies, waits for them, and re-layouts  2.91 us

profile of v6, /device:TPU:1, one launch (start us, length us, event | category | flops | bytes accessed | tf_op | source)
XLA Modules:
  0.0 67.5 jit_solution(4650794769225085872)
XLA Ops:
  1.9 0.0 copy-start
  1.9 0.8 %copy-done = bf16[18,1152]{1,0:T(8,128)(2,1)S(1)} copy-done((bf16[18,1152]{1,0:T(8,128)(2,1)S(1)}, bf16[18,1152]{1,0:T(8,128)(2,1)}, u32[]{:S(2)}) %copy-start) | copy-done | bytes 41496
  2.7 0.0 copy-start.1
  2.7 0.8 %copy-done.1 = bf16[288,72]{0,1:T(8,128)(2,1)S(1)} copy-done((bf16[288,72]{0,1:T(8,128)(2,1)S(1)}, bf16[288,72]{0,1:T(8,128)(2,1)}, u32[]{:S(2)}) %copy-start.1) | copy-done | bytes 41496
  3.6 62.1 %siglip.1 = (f32[8,128]{1,0:T(8,128)S(1)}, f32[18,1152]{1,0:T(8,128)S(1)}, f32[72,288]{1,0:T(8,128)S(1)}) custom-call(bf16[18,1152]{1,0:T(8,128)(2,1)S(1)} %copy-done, bf16[72,288]{1,0:T(8,128)(2,1)S(1)} %bitcast.4, f32[1]{0:T(128)S(6)} %copy.9.scale, f32[1]{0:T(128)S(6)} %copy.10.bias), custom_call_target="tpu_custom_call" | custom-call | tf_op jit(solution)/shard_map/siglip/pallas_call | solution.py:452
  65.7 0.5 slice.3
  66.2 0.6 copy.11
  66.8 0.6 copy.12
Async XLA Ops:
  1.9 0.8 %copy-start = (bf16[18,1152]{1,0:T(8,128)(2,1)S(1)}, bf16[18,1152]{1,0:T(8,128)(2,1)}, u32[]{:S(2)}) copy-start(bf16[18,1152]{1,0:T(8,128)(2,1)} %images.1) | copy-start | bytes 124420
  2.7 0.8 %copy-start.1 = (bf16[288,72]{0,1:T(8,128)(2,1)S(1)}, bf16[288,72]{0,1:T(8,128)(2,1)}, u32[]{:S(2)}) copy-start(bf16[288,72]{0,1:T(8,128)(2,1)} %param.5) | copy-start | bytes 124420
